TPU v7x, 128 devices: a whole 4x4x4 slice. The times are simulated.
128 devices in a mesh: dp: 8 (over y, x_lo), ctx: 16 (over x_hi, z, core).
Axes of the slice: x: 4 (x_hi: 2, x_lo: 2; x = x_hi * 2 + x_lo), y: 4, z: 4, core: 2. Of those that a mesh axis runs over, the one named last changes fastest.
Arguments:
- proj: bfloat16 [32768, 3072], P(('dp', 'ctx')), may hold values from -6 to 6
- short_w: float32 [3, 3072], replicated, may hold values from -3.5 to 3.5
- filt: float32 [4096, 1024], P(None, 'ctx'), may hold values from -4 to 4
- skip_gain: float32 [1024], replicated, may hold values from -1 to 1
- cotangent: bfloat16 [32768, 1024], P(('dp', 'ctx')), may hold values from -6 to 6
Outputs:
- outputs: bfloat16 [32768, 1024], P(('dp', 'ctx'))
- proj_grad: bfloat16 [32768, 3072], P(('dp', 'ctx'))
- short_grad: float32 [3, 3072], replicated
- skip_grad: float32 [1024], replicated
- filt_grad: float32 [4096, 1024], P('dp', 'ctx')
All inputs are finite; a program needn't handle non-finite values.
Results may differ from a plain program's by a relative error of at most 0.017.
Values may be sent and summed in bfloat16 or wider, within the bound.
A program may use at most 128 MiB of HBM per device.

v0:
```python
import functools
import math

import jax
import jax.numpy as jnp
import ml_dtypes
import numpy as np
from jax import lax
from jax.experimental import pallas as pl
from jax.experimental.pallas import tpu as pltpu
from jax.sharding import PartitionSpec as P

HI = 256
LO = 16
GROUP = 8
GROUPS = HI // GROUP
LANES = 128
HALF = 64
MESH = pl.DeviceIdType.MESH
F32 = jnp.float32
BF16 = jnp.bfloat16


def tables():
    total = HI * LO
    start = np.arange(HI)
    angle = 2.0 * math.pi / HI * ((start[:, None] + 0.25) * np.arange(HI)[None, :] % HI)
    first = np.stack([np.cos(angle), -np.sin(angle)])
    first = first.reshape(2, GROUPS, GROUP, HI).transpose(1, 0, 2, 3).reshape(2 * HI, HI)
    freq = HI * np.arange(LO)[None, None, :] + start.reshape(GROUPS, GROUP)[:, :, None] + 0.25
    angle = 2.0 * math.pi / total * (freq[..., None] * np.arange(LO) % total)
    second = np.zeros((GROUPS, 2, LO, GROUP, LO, 2, GROUP))
    for at in range(GROUP):
        second[:, 0, :, at, :, 0, at] = np.cos(angle[:, at])
        second[:, 0, :, at, :, 1, at] = np.sin(angle[:, at])
        second[:, 1, :, at, :, 0, at] = -np.sin(angle[:, at])
        second[:, 1, :, at, :, 1, at] = np.cos(angle[:, at])
    second = second.reshape(GROUPS, 2 * LO * GROUP, 2 * LO * GROUP)
    rows = np.arange(256)
    perm = np.zeros((256, 256))
    perm[rows, rows % 16 * LO + rows // 16] = 1.0
    return [
        table.astype(ml_dtypes.bfloat16)
        for table in (perm, perm.T, first, second, first.T / total, second.transpose(0, 2, 1))
    ]


def dot(left, right):
    return jnp.dot(left, right, preferred_element_type=F32)


def low_lanes(rows):
    return lax.broadcasted_iota(jnp.int32, (rows, LANES), 1) < HALF


def delayed(x, rim, steps):
    turned = pltpu.roll(x, steps, 0)
    before = pltpu.roll(rim, steps, 0)
    row = lax.broadcasted_iota(jnp.int32, (8, LANES), 0)
    return jnp.concatenate([jnp.where(row < steps, before, turned[:8]), turned[8:]], axis=0)


def advanced(x, steps):
    rows = x.shape[0]
    turned = pltpu.roll(x, rows - steps, 0)
    row = lax.broadcasted_iota(jnp.int32, (8, LANES), 0)
    return jnp.concatenate(
        [turned[: rows - 8], jnp.where(row < 8 - steps, turned[rows - 8 :], 0.0)], axis=0
    )


def kernel(
    scale,
    proj_h, cot_h, filt_h, short_h, skip_h, perm_h, unperm_h, first_h, second_h, firstt_h, secondt_h,
    out_h, pg_h, sg_h, skg_h, fg_h,
    proj_v, cot_v, filt_v, short_v, skip_v, perm_v, unperm_v, first_v, second_v, firstt_v, secondt_v,
    rim_v, mix_v, send_v, recv_v, fx_v, y_v, fs_v, z_v, ysend_v, brecv_v, fsend_v, frecv_v,
    out_v, pg_v, tail_v, rsend_v, rrecv_v, asend_v, arecv_v, dsend_v, drecv_v, gsend_v, grecv_v,
    sg_v, skg_v, fg_v,
    load_sem, rim_ss, rim_rs, a_ss, a_rs, b_ss, b_rs, f_ss, f_rs, r_ss, r_rs, s_ss, s_rs, d_ss, d_rs,
    g_ss, g_rs, local_sem, store_sem,
):
    me = lax.axis_index("ctx")
    dpi = lax.axis_index("dp")
    chip = me // 2
    nxt = lax.rem(me + 1, 16)
    prv = lax.rem(me + 15, 16)

    barrier = pltpu.get_barrier_semaphore()
    for step in range(1, 16):
        pl.semaphore_signal(
            barrier, inc=1, device_id={"ctx": lax.rem(me + step, 16)}, device_id_type=MESH
        )
    for step in range(1, 8):
        pl.semaphore_signal(
            barrier, inc=1, device_id={"dp": lax.rem(dpi + step, 8)}, device_id_type=MESH
        )

    loads = [
        pltpu.make_async_copy(src, dst, load_sem.at[at])
        for at, (src, dst) in enumerate(
            [
                (proj_h, proj_v), (cot_h, cot_v), (short_h, short_v), (perm_h, perm_v), (filt_h, filt_v),
                (first_h, first_v), (second_h, second_v), (secondt_h, secondt_v), (firstt_h, firstt_v),
                (unperm_h, unperm_v), (skip_h, skip_v),
            ]
        )
    ]
    for load in loads:
        load.start()
    asend_v[...] = jnp.zeros_like(asend_v)
    pl.semaphore_wait(barrier, 22)

    def rim_copy(to):
        return pltpu.make_async_remote_copy(
            src_ref=proj_h.at[pl.ds(240, 16), :], dst_ref=rim_v, send_sem=rim_ss.at[0], recv_sem=rim_rs.at[0],
            device_id={"ctx": to}, device_id_type=MESH,
        )

    rim_copy(nxt).start()
    for load in loads[:4]:
        load.wait()
    rim_copy(nxt).wait()
    keep = jnp.where(me == 0, 0.0, 1.0).astype(F32)

    def forward_copy(to, source):
        return pltpu.make_async_remote_copy(
            src_ref=send_v.at[to], dst_ref=recv_v.at[:, pl.ds(pl.multiple_of(source * 16, 16), 16), :],
            send_sem=a_ss.at[to], recv_sem=a_rs.at[source], device_id={"ctx": to}, device_id_type=MESH,
        )

    def gate_tile(step, carry):
        tile = lax.rem(chip + step, 8)
        cols = pl.ds(pl.multiple_of(tile * LANES, LANES), LANES)
        mixed = []
        for part in range(3):
            cut = pl.ds(pl.multiple_of(tile * LANES + part * 1024, LANES), LANES)
            x = proj_v[:, cut].astype(F32)
            rim = rim_v[:, cut].astype(F32)[8:16] * keep
            w = short_v[:, cut]
            value = w[0:1] * x + w[1:2] * delayed(x, rim, 1) + w[2:3] * delayed(x, rim, 2)
            mix_v[part, :, cols] = value
            mixed.append(value)
        product = (mixed[1] * mixed[2]).astype(BF16)
        grad = (cot_v[:, cols].astype(F32) * mixed[0]).astype(BF16)
        both = dot(perm_v[...], jnp.concatenate([product, grad], axis=1))
        p, g = both[:, :LANES], both[:, LANES:]
        low = low_lanes(256)
        even = jnp.where(low, p, pltpu.roll(g, HALF, 1))
        odd = jnp.where(low, pltpu.roll(p, HALF, 1), g)
        send_v[2 * tile] = even.astype(BF16).reshape(16, 16, LANES)
        send_v[2 * tile + 1] = odd.astype(BF16).reshape(16, 16, LANES)
        for core in range(2):

            @pl.when(2 * tile + core != me)
            def _():
                forward_copy(2 * tile + core, me).start()

        return carry

    lax.fori_loop(1, 9, gate_tile, 0)
    own = pltpu.make_async_copy(
        send_v.at[me], recv_v.at[:, pl.ds(pl.multiple_of(me * 16, 16), 16), :], local_sem.at[0]
    )
    own.start()

    def first_stage(source, pair, carry):
        x = jnp.concatenate([source[2 * pair], source[2 * pair + 1]], axis=1)
        y = dot(first_v[...], x).astype(BF16)
        y_v[2 * pair] = y[:, :LANES]
        y_v[2 * pair + 1] = y[:, LANES:]
        return carry

    def second_stage(group):
        rows = y_v[:, pl.ds(pl.multiple_of(group * 16, 16), 16), :].reshape(256, LANES)
        return dot(second_v[group], rows)

    for load in loads[4:7]:
        load.wait()

    def filter_rows(block, carry):
        x = filt_v[pl.ds(pl.multiple_of(block * 256, 256), 256), :]
        x = jnp.concatenate([x, x], axis=1).astype(BF16)
        x = dot(perm_v[...], x).astype(BF16).reshape(16, 16, LANES)
        fx_v[:, pl.ds(pl.multiple_of(block * 16, 16), 16), :] = x
        return carry

    def filter_group(group, carry):
        spec = second_stage(group)
        fs_v[group, :LANES] = spec[:LANES]
        fs_v[group, LANES:] = jnp.where(low_lanes(LANES), spec[LANES:], -spec[LANES:])
        return carry

    lax.fori_loop(0, 16, filter_rows, 0)
    lax.fori_loop(0, 8, functools.partial(first_stage, fx_v), 0)
    lax.fori_loop(0, GROUPS, filter_group, 0)
    for load in loads[7:]:
        load.wait()

    own.wait()

    def wait_forward(step, carry):
        forward_copy(me, lax.rem(me + step, 16)).wait_recv()
        return carry

    lax.fori_loop(1, 16, wait_forward, 0)

    lax.fori_loop(0, 8, functools.partial(first_stage, recv_v), 0)

    def middle_group(group, carry):
        spec = second_stage(group)
        sr, si = spec[:LANES], spec[LANES:]
        fr, fi = fs_v[group, :LANES], fs_v[group, LANES:]
        rr, ri = pltpu.roll(sr, HALF, 1), pltpu.roll(si, HALF, 1)
        cross = ri * sr - rr * si
        low = low_lanes(LANES)
        real = jnp.concatenate([sr * fr - si * fi, sr * rr + si * ri], axis=1)
        imag = jnp.concatenate([sr * fi + si * fr, jnp.where(low, cross, -cross)], axis=1)
        freq = jnp.concatenate([real, imag], axis=0).astype(BF16)
        back = dot(secondt_v[group], freq).astype(BF16).reshape(16, 16, 2 * LANES)
        z_v[:, pl.ds(pl.multiple_of(group * 16, 16), 16), :] = back
        return carry

    lax.fori_loop(0, GROUPS, middle_group, 0)

    def last_stage(pair, carry):
        even = dot(firstt_v[...], z_v[2 * pair])
        odd = dot(firstt_v[...], z_v[2 * pair + 1])
        ysend_v[2 * pair] = even[:, :LANES].astype(BF16)
        ysend_v[2 * pair + 1] = odd[:, :LANES].astype(BF16)
        grad = jnp.where(low_lanes(256), even[:, LANES:], odd[:, LANES:]) * scale
        fsend_v[pair] = grad.astype(BF16)
        return carry

    def back_copy(to, source, half):
        return pltpu.make_async_remote_copy(
            src_ref=ysend_v.at[pl.ds(half * 8, 8), pl.ds(pl.multiple_of(to * 16, 16), 16), :],
            dst_ref=brecv_v.at[source, pl.ds(half * 8, 8)],
            send_sem=b_ss.at[half, to], recv_sem=b_rs.at[half, source],
            device_id={"ctx": to}, device_id_type=MESH,
        )

    for half in range(2):
        lax.fori_loop(4 * half, 4 * half + 4, last_stage, 0)

        def send_back(step, carry, half=half):
            back_copy(lax.rem(me + step, 16), me, half).start()
            return carry

        lax.fori_loop(1, 16, send_back, 0)

    def filter_copy(to, source):
        return pltpu.make_async_remote_copy(
            src_ref=fsend_v.at[:, pl.ds(pl.multiple_of(to * 32, 32), 32), :], dst_ref=frecv_v.at[source],
            send_sem=f_ss.at[to], recv_sem=f_rs.at[source], device_id={"dp": to}, device_id_type=MESH,
        )

    def send_filter(step, carry):
        filter_copy(lax.rem(dpi + step, 8), dpi).start()
        return carry

    lax.fori_loop(1, 8, send_filter, 0)
    own_back = pltpu.make_async_copy(
        ysend_v.at[:, pl.ds(pl.multiple_of(me * 16, 16), 16), :], brecv_v.at[me], local_sem.at[1]
    )
    own_back.start()
    own_filter = pltpu.make_async_copy(
        fsend_v.at[:, pl.ds(pl.multiple_of(dpi * 32, 32), 32), :], frecv_v.at[dpi], local_sem.at[2]
    )
    own_filter.start()
    own_back.wait()
    own_filter.wait()

    def rim_back_copy(tile, to):
        return pltpu.make_async_remote_copy(
            src_ref=rsend_v.at[tile], dst_ref=rrecv_v.at[tile], send_sem=r_ss.at[tile], recv_sem=r_rs.at[tile],
            device_id={"ctx": to}, device_id_type=MESH,
        )

    def sum_copy(to, source):
        return pltpu.make_async_remote_copy(
            src_ref=asend_v.at[to], dst_ref=arecv_v.at[source], send_sem=s_ss.at[to], recv_sem=s_rs.at[source],
            device_id={"ctx": to}, device_id_type=MESH,
        )

    def down(x):
        return jnp.sum(x, axis=0, keepdims=True)

    def grad_tile(step, carry):
        tile = lax.rem(chip + step, 8)
        cols = pl.ds(pl.multiple_of(tile * LANES, LANES), LANES)
        for core in range(2):

            @pl.when(2 * tile + core != me)
            def _():
                back_copy(me, 2 * tile + core, 0).wait_recv()
                back_copy(me, 2 * tile + core, 1).wait_recv()

        pair = jnp.concatenate(
            [brecv_v[2 * tile].reshape(256, LANES), brecv_v[2 * tile + 1].reshape(256, LANES)], axis=1
        )
        pair = dot(unperm_v[...], pair)
        even, odd = pair[:, :LANES], pair[:, LANES:]
        low = low_lanes(256)
        long_part = jnp.where(low, even, pltpu.roll(odd, HALF, 1))
        back_part = jnp.where(low, pltpu.roll(even, HALF, 1), odd)
        queries, keys, values = (mix_v[part, :, cols] for part in range(3))
        cot = cot_v[:, cols].astype(F32)
        gain = skip_v[:, cols]
        product = (keys * values).astype(BF16).astype(F32)
        grad = (cot * queries).astype(BF16).astype(F32)
        gated = long_part + gain * product
        out_v[:, cols] = (queries * gated).astype(BF16)
        product_grad = back_part + gain * grad
        for part, mixed_grad in enumerate((cot * gated, product_grad * values, product_grad * keys)):
            cut = pl.ds(pl.multiple_of(tile * LANES + part * 1024, LANES), LANES)
            rounded = mixed_grad.astype(BF16)
            rsend_v[tile, 16 * part : 16 * part + 16] = rounded[:16]
            mg = rounded.astype(F32)
            one, two = advanced(mg, 1), advanced(mg, 2)
            w = short_v[:, cut]
            value = w[0:1] * mg + w[1:2] * one + w[2:3] * two
            pg_v[:, cut] = value.astype(BF16)
            tail_v[tile, 16 * part : 16 * part + 16] = value[240:]
            x = proj_v[:, cut].astype(F32)
            rim = rim_v[:, cut].astype(F32)[8:16] * keep
            head = mg[:8]
            sums = [
                down(mg * x),
                down(one * x) + head[0:1] * rim[7:8],
                down(two * x) + head[0:1] * rim[6:7] + head[1:2] * rim[7:8],
            ]
            for tap in range(3):
                at = 3 * part + tap
                asend_v[2 * tile + at // 8, at % 8 : at % 8 + 1] = sums[tap]
        asend_v[2 * tile + 1, 1:2] = down(grad * product)
        rim_back_copy(tile, prv).start()
        for core in range(2):

            @pl.when(2 * tile + core != me)
            def _():
                sum_copy(2 * tile + core, me).start()

        return carry

    lax.fori_loop(1, 9, grad_tile, 0)
    arecv_v[me] = asend_v[me]
    stores = [
        pltpu.make_async_copy(out_v, out_h, store_sem.at[0]),
        pltpu.make_async_copy(pg_v.at[pl.ds(0, 240)], pg_h.at[pl.ds(0, 240)], store_sem.at[1]),
    ]
    for store in stores:
        store.start()

    def wait_sums(step, carry):
        sum_copy(me, lax.rem(me + step, 16)).wait_recv()
        return carry

    lax.fori_loop(1, 16, wait_sums, 0)
    total = arecv_v[0]
    for at in range(1, 16):
        total = total + arecv_v[at]
    dsend_v[...] = total
    drecv_v[dpi] = total

    def part_copy(to, source):
        return pltpu.make_async_remote_copy(
            src_ref=dsend_v, dst_ref=drecv_v.at[source], send_sem=d_ss.at[to], recv_sem=d_rs.at[source],
            device_id={"dp": to}, device_id_type=MESH,
        )

    def all_copy(to, source):
        return pltpu.make_async_remote_copy(
            src_ref=gsend_v, dst_ref=grecv_v.at[source], send_sem=g_ss.at[to], recv_sem=g_rs.at[source],
            device_id={"ctx": to}, device_id_type=MESH,
        )

    def send_part(step, carry):
        part_copy(lax.rem(dpi + step, 8), dpi).start()
        return carry

    lax.fori_loop(1, 8, send_part, 0)

    def wait_filter(step, carry):
        filter_copy(dpi, lax.rem(dpi + step, 8)).wait_recv()
        return carry

    lax.fori_loop(1, 8, wait_filter, 0)
    for pair in range(8):
        value = frecv_v[0, pair].astype(F32)
        for at in range(1, 8):
            value = value + frecv_v[at, pair].astype(F32)
        fg_v[pl.ds(2 * pair, 32, 16), :] = value[:, :HALF]
        fg_v[pl.ds(2 * pair + 1, 32, 16), :] = pltpu.roll(value, HALF, 1)[:, :HALF]
    store = pltpu.make_async_copy(fg_v, fg_h, store_sem.at[2])
    store.start()
    stores.append(store)

    def wait_part(step, carry):
        part_copy(dpi, lax.rem(dpi + step, 8)).wait_recv()
        return carry

    lax.fori_loop(1, 8, wait_part, 0)
    total = drecv_v[0]
    for at in range(1, 8):
        total = total + drecv_v[at]
    total = total * scale
    gsend_v[...] = total
    grecv_v[me] = total

    def send_all(step, carry):
        all_copy(lax.rem(me + step, 16), me).start()
        return carry

    lax.fori_loop(1, 16, send_all, 0)

    keep_back = jnp.where(me == 15, 0.0, 1.0).astype(F32)

    def fix_tile(tile, carry):
        rim_back_copy(tile, prv).wait_recv()
        row = lax.broadcasted_iota(jnp.int32, (16, LANES), 0)
        for part in range(3):
            cut = pl.ds(pl.multiple_of(tile * LANES + part * 1024, LANES), LANES)
            rim = rrecv_v[tile, 16 * part : 16 * part + 16].astype(F32) * keep_back
            w = short_v[:, cut]
            value = tail_v[tile, 16 * part : 16 * part + 16]
            value = value + jnp.where(row == 15, w[1:2] * rim[0:1] + w[2:3] * rim[1:2], 0.0)
            value = value + jnp.where(row == 14, w[2:3] * rim[0:1], 0.0)
            pg_v[pl.ds(240, 16), cut] = value.astype(BF16)
        return carry

    lax.fori_loop(0, 8, fix_tile, 0)
    store = pltpu.make_async_copy(pg_v.at[pl.ds(240, 16)], pg_h.at[pl.ds(240, 16)], store_sem.at[3])
    store.start()
    stores.append(store)

    def wait_all(step, carry):
        all_copy(me, lax.rem(me + step, 16)).wait_recv()
        return carry

    lax.fori_loop(1, 16, wait_all, 0)
    for tile in range(8):
        for at in range(9):
            part, tap = at // 3, at % 3
            left = part * 1024 + tile * LANES
            sg_v[tap : tap + 1, left : left + LANES] = grecv_v[2 * tile + at // 8, at % 8 : at % 8 + 1]
        skg_v[:, tile * LANES : tile * LANES + LANES] = grecv_v[2 * tile + 1, 1:2]
    for at, (src, dst) in enumerate([(sg_v, sg_h), (skg_v, skg_h)]):
        store = pltpu.make_async_copy(src, dst, store_sem.at[4 + at])
        store.start()
        stores.append(store)

    def wait_sends(step, carry):
        to = lax.rem(me + step, 16)
        forward_copy(to, me).wait_send()
        back_copy(to, me, 0).wait_send()
        back_copy(to, me, 1).wait_send()
        sum_copy(to, me).wait_send()
        all_copy(to, me).wait_send()
        return carry

    def wait_dp_sends(step, carry):
        to = lax.rem(dpi + step, 8)
        filter_copy(to, dpi).wait_send()
        part_copy(to, dpi).wait_send()
        return carry

    def wait_rim_sends(tile, carry):
        rim_back_copy(tile, prv).wait_send()
        return carry

    lax.fori_loop(1, 16, wait_sends, 0)
    lax.fori_loop(1, 8, wait_dp_sends, 0)
    lax.fori_loop(0, 8, wait_rim_sends, 0)
    for store in stores:
        store.wait()


def shards(proj, short_w, filt, skip_gain, cotangent):
    width = skip_gain.shape[0]
    scale = 1.0 / math.sqrt(proj.shape[0] * lax.axis_size("dp") * lax.axis_size("ctx"))
    whole = pl.BlockSpec(memory_space=pl.ANY)
    dma = pltpu.SemaphoreType.DMA
    outs = pl.pallas_call(
        functools.partial(kernel, scale),
        out_shape=[
            jax.ShapeDtypeStruct((256, 1024), BF16),
            jax.ShapeDtypeStruct((256, 3072), BF16),
            jax.ShapeDtypeStruct((3, 3072), F32),
            jax.ShapeDtypeStruct((1, 1024), F32),
            jax.ShapeDtypeStruct((512, HALF), F32),
        ],
        in_specs=[whole] * 11,
        out_specs=[whole] * 5,
        scratch_shapes=[
            pltpu.VMEM((256, 3072), BF16),
            pltpu.VMEM((256, 1024), BF16),
            pltpu.VMEM((4096, HALF), F32),
            pltpu.VMEM((3, 3072), F32),
            pltpu.VMEM((1, 1024), F32),
            pltpu.VMEM((256, 256), BF16),
            pltpu.VMEM((256, 256), BF16),
            pltpu.VMEM((2 * HI, HI), BF16),
            pltpu.VMEM((GROUPS, 256, 256), BF16),
            pltpu.VMEM((HI, 2 * HI), BF16),
            pltpu.VMEM((GROUPS, 256, 256), BF16),
            pltpu.VMEM((16, 3072), BF16),
            pltpu.VMEM((3, 256, 1024), F32),
            pltpu.VMEM((16, 16, 16, LANES), BF16),
            pltpu.VMEM((LO, HI, LANES), BF16),
            pltpu.VMEM((LO, HI, LANES), BF16),
            pltpu.VMEM((LO, 2 * HI, LANES), BF16),
            pltpu.VMEM((GROUPS, 256, LANES), F32),
            pltpu.VMEM((LO, 2 * HI, 2 * LANES), BF16),
            pltpu.VMEM((LO, HI, LANES), BF16),
            pltpu.VMEM((16, LO, 16, LANES), BF16),
            pltpu.VMEM((8, HI, LANES), BF16),
            pltpu.VMEM((8, 8, 32, LANES), BF16),
            pltpu.VMEM((256, 1024), BF16),
            pltpu.VMEM((256, 3072), BF16),
            pltpu.VMEM((8, 48, LANES), F32),
            pltpu.VMEM((8, 48, LANES), BF16),
            pltpu.VMEM((8, 48, LANES), BF16),
            pltpu.VMEM((16, 8, LANES), F32),
            pltpu.VMEM((16, 8, LANES), F32),
            pltpu.VMEM((8, LANES), F32),
            pltpu.VMEM((8, 8, LANES), F32),
            pltpu.VMEM((8, LANES), F32),
            pltpu.VMEM((16, 8, LANES), F32),
            pltpu.VMEM((3, 3072), F32),
            pltpu.VMEM((1, 1024), F32),
            pltpu.VMEM((512, HALF), F32),
            dma((11,)),
            dma((1,)), dma((1,)), dma((16,)), dma((16,)), dma((2, 16)), dma((2, 16)), dma((8,)), dma((8,)),
            dma((8,)), dma((8,)), dma((16,)), dma((16,)), dma((8,)), dma((8,)), dma((16,)), dma((16,)),
            dma((3,)), dma((6,)),
        ],
        compiler_params=pltpu.CompilerParams(
            collective_id=0, has_side_effects=True, vmem_limit_bytes=56 * 1024 * 1024
        ),
    )(proj, cotangent, filt, short_w, skip_gain.reshape(1, width), *tables())
    outputs, proj_grad, short_grad, skip_grad, filt_grad = outs
    return (outputs, proj_grad, short_grad, skip_grad.reshape(width), filt_grad)


def solution(mesh):
    placed = (P(("dp", "ctx"), None), P(), P(None, "ctx"), P(), P(("dp", "ctx"), None))
    return jax.shard_map(
        shards,
        mesh=mesh,
        in_specs=placed,
        out_specs=(P(("dp", "ctx"), None), P(("dp", "ctx"), None), P(), P(), P("dp", "ctx")),
        check_vma=False,
    )
```

profile of v0, /device:TPU:1, one launch (start us, length us, event | category | flops | bytes accessed | tf_op | source)
XLA Modules:
  0.0 90.9 jit_solution(4472223420976543228)
XLA Ops:
  0.6 3.2 %copy.16.filt_h = f32[4096,64]{1,0:T(8,128)} copy(f32[4096,64]{0,1:T(8,128)} %param.13) | data formatting | bytes 2097152 | tf_op args[2]
  3.8 79.6 %shard_map.146 = (bf16[256,1024]{1,0:T(8,128)(2,1)}, bf16[256,3072]{1,0:T(8,128)(2,1)}, f32[3,3072]{1,0:T(4,128)}, f32[1,1024]{1,0:T(1,128)}, f32[512,64]{1,0:T(8,128)}) custom-call(bf16[256,3072]{1,0:T(8,128)(2,1)} %proj_h.1, bf16[256,1024]{1,0:T(8,128)(2,1)} %cot_h.1, f32[4096,64]{1,0:T(8,128)} %copy.16.filt_h, f32[3,3072]{1,0:T(4,128)} %short_h.1, ...), custom_call_target="tpu_custom_call" | custom-call | tf_op jit(solution)/shard_map/pallas_call | solution.py:484
  83.4 1.7 %copy.17 = f32[512,64]{0,1:T(8,128)} copy(f32[512,64]{1,0:T(8,128)} %get-tuple-element.19) | data formatting | bytes 262144
  85.2 0.0 copy-start
  85.2 0.0 copy-start.1
  85.2 1.9 %copy.22 = bf16[256,1024]{1,0:T(8,128)(2,1)} copy(bf16[256,1024]{1,0:T(8,128)(2,1)} %get-tuple-element.25) | data formatting | bytes 1048576
  87.0 2.7 %copy.23 = bf16[256,3072]{1,0:T(8,128)(2,1)} copy(bf16[256,3072]{1,0:T(8,128)(2,1)} %get-tuple-element.26) | data formatting | bytes 3145728
  89.7 0.0 copy-done
  89.7 0.6 copy.24
  90.3 0.0 copy-done.1
  90.3 0.6 copy.25
Async XLA Ops:
  85.2 4.5 %copy-start = (f32[3,3072]{1,0:T(4,128)S(1)}, f32[3,3072]{1,0:T(4,128)}, u32[]{:S(2)}) copy-start(f32[3,3072]{1,0:T(4,128)} %get-tuple-element.27) | copy-start | bytes 110596
  85.2 5.2 %copy-start.1 = (f32[1,1024]{1,0:T(1,128)S(1)}, f32[1,1024]{1,0:T(1,128)}, u32[]{:S(2)}) copy-start(f32[1,1024]{1,0:T(1,128)} %get-tuple-element.13) | copy-start | bytes 12292
where the time goes:
time: 91.1 us; the launch traced here: 90.9 us
  Pallas kernels  79.6 us (87%)
  local copies, waits for them, and re-layouts  10.6 us (12%)
    pallas_call x1, Pallas kernels, shards(): pl.pallas_call(functools.partial(kernel, scale), out_shape=[jax.ShapeDtyp...  79.6 us
    unnamed x10, local copies, waits for them, and re-layouts  10.6 us

commit v1 on v0

--- a/solution.py
+++ b/solution.py
@@ -14,6 +14,7 @@
 LO = 16
 GROUP = 8
 GROUPS = HI // GROUP
+UNROLL = 4
 LANES = 128
 HALF = 64
 MESH = pl.DeviceIdType.MESH
@@ -72,13 +73,12 @@
 def kernel(
     scale,
     proj_h, cot_h, filt_h, short_h, skip_h, perm_h, unperm_h, first_h, second_h, firstt_h, secondt_h,
-    out_h, pg_h, sg_h, skg_h, fg_h,
+    out_v, pg_v, sg_v, skg_v, fg_v,
     proj_v, cot_v, filt_v, short_v, skip_v, perm_v, unperm_v, first_v, second_v, firstt_v, secondt_v,
-    rim_v, mix_v, send_v, recv_v, fx_v, y_v, fs_v, z_v, ysend_v, brecv_v, fsend_v, frecv_v,
-    out_v, pg_v, tail_v, rsend_v, rrecv_v, asend_v, arecv_v, dsend_v, drecv_v, gsend_v, grecv_v,
-    sg_v, skg_v, fg_v,
-    load_sem, rim_ss, rim_rs, a_ss, a_rs, b_ss, b_rs, f_ss, f_rs, r_ss, r_rs, s_ss, s_rs, d_ss, d_rs,
-    g_ss, g_rs, local_sem, store_sem,
+    rim_v, mix_v, send_v, recv_v, fx_v, y_v, fs_v, spec_v, z_v, ysend_v, brecv_v, fsend_v, frecv_v, hsend_v, hrecv_v,
+    tail_v, rsend_v, rrecv_v, asend_v, arecv_v, dsend_v, drecv_v, gsend_v, grecv_v, wide_v,
+    load_sem, rim_ss, rim_rs, a_ss, a_rs, b_ss, b_rs, f_ss, f_rs, h_ss, h_rs, r_ss, r_rs, s_ss, s_rs, d_ss, d_rs,
+    g_ss, g_rs, local_sem,
 ):
     me = lax.axis_index("ctx")
     dpi = lax.axis_index("dp")
@@ -126,7 +126,7 @@
     def forward_copy(to, source):
         return pltpu.make_async_remote_copy(
             src_ref=send_v.at[to], dst_ref=recv_v.at[:, pl.ds(pl.multiple_of(source * 16, 16), 16), :],
-            send_sem=a_ss.at[to], recv_sem=a_rs.at[source], device_id={"ctx": to}, device_id_type=MESH,
+            send_sem=a_ss.at[0], recv_sem=a_rs.at[0], device_id={"ctx": to}, device_id_type=MESH,
         )
 
     def gate_tile(step, carry):
@@ -179,9 +179,10 @@
         load.wait()
 
     def filter_rows(block, carry):
-        x = filt_v[pl.ds(pl.multiple_of(block * 256, 256), 256), :]
-        x = jnp.concatenate([x, x], axis=1).astype(BF16)
-        x = dot(perm_v[...], x).astype(BF16).reshape(16, 16, LANES)
+        x = filt_v[:, pl.ds(pl.multiple_of(block * 256, 256), 256)].astype(BF16)
+        x = jnp.concatenate([x, x], axis=0)
+        x = lax.dot_general(perm_v[...], x, (((1,), (1,)), ((), ())), preferred_element_type=F32)
+        x = x.astype(BF16).reshape(16, 16, LANES)
         fx_v[:, pl.ds(pl.multiple_of(block * 16, 16), 16), :] = x
         return carry
 
@@ -193,51 +194,50 @@
 
     lax.fori_loop(0, 16, filter_rows, 0)
     lax.fori_loop(0, 8, functools.partial(first_stage, fx_v), 0)
-    lax.fori_loop(0, GROUPS, filter_group, 0)
+    lax.fori_loop(0, GROUPS, filter_group, 0, unroll=UNROLL)
     for load in loads[7:]:
         load.wait()
 
     own.wait()
 
-    def wait_forward(step, carry):
-        forward_copy(me, lax.rem(me + step, 16)).wait_recv()
-        return carry
-
-    lax.fori_loop(1, 16, wait_forward, 0)
+    whole_forward = pltpu.make_async_remote_copy(
+        src_ref=send_v.at[pl.ds(0, 15)], dst_ref=recv_v.at[:, pl.ds(0, 240), :],
+        send_sem=a_ss.at[0], recv_sem=a_rs.at[0], device_id={"ctx": nxt}, device_id_type=MESH,
+    )
+    whole_forward.wait_recv()
 
     lax.fori_loop(0, 8, functools.partial(first_stage, recv_v), 0)
 
     def middle_group(group, carry):
         spec = second_stage(group)
+        spec_v[group] = spec.astype(BF16)
         sr, si = spec[:LANES], spec[LANES:]
         fr, fi = fs_v[group, :LANES], fs_v[group, LANES:]
-        rr, ri = pltpu.roll(sr, HALF, 1), pltpu.roll(si, HALF, 1)
-        cross = ri * sr - rr * si
-        low = low_lanes(LANES)
-        real = jnp.concatenate([sr * fr - si * fi, sr * rr + si * ri], axis=1)
-        imag = jnp.concatenate([sr * fi + si * fr, jnp.where(low, cross, -cross)], axis=1)
-        freq = jnp.concatenate([real, imag], axis=0).astype(BF16)
-        back = dot(secondt_v[group], freq).astype(BF16).reshape(16, 16, 2 * LANES)
+        freq = jnp.concatenate([sr * fr - si * fi, sr * fi + si * fr], axis=0).astype(BF16)
+        back = dot(secondt_v[group], freq).astype(BF16).reshape(16, 16, LANES)
         z_v[:, pl.ds(pl.multiple_of(group * 16, 16), 16), :] = back
         return carry
 
-    lax.fori_loop(0, GROUPS, middle_group, 0)
+    lax.fori_loop(0, GROUPS, middle_group, 0, unroll=UNROLL)
 
     def last_stage(pair, carry):
-        even = dot(firstt_v[...], z_v[2 * pair])
-        odd = dot(firstt_v[...], z_v[2 * pair + 1])
-        ysend_v[2 * pair] = even[:, :LANES].astype(BF16)
-        ysend_v[2 * pair + 1] = odd[:, :LANES].astype(BF16)
-        grad = jnp.where(low_lanes(256), even[:, LANES:], odd[:, LANES:]) * scale
-        fsend_v[pair] = grad.astype(BF16)
+        both = jnp.concatenate([z_v[2 * pair], z_v[2 * pair + 1]], axis=1)
+        both = dot(firstt_v[...], both).astype(BF16)
+        ysend_v[2 * pair] = both[:, :LANES]
+        ysend_v[2 * pair + 1] = both[:, LANES:]
         return carry
 
     def back_copy(to, source, half):
         return pltpu.make_async_remote_copy(
             src_ref=ysend_v.at[pl.ds(half * 8, 8), pl.ds(pl.multiple_of(to * 16, 16), 16), :],
             dst_ref=brecv_v.at[source, pl.ds(half * 8, 8)],
-            send_sem=b_ss.at[half, to], recv_sem=b_rs.at[half, source],
-            device_id={"ctx": to}, device_id_type=MESH,
+            send_sem=b_ss.at[0], recv_sem=b_rs.at[source], device_id={"ctx": to}, device_id_type=MESH,
+        )
+
+    def whole_back(source):
+        return pltpu.make_async_remote_copy(
+            src_ref=ysend_v.at[:, pl.ds(0, 240), :], dst_ref=brecv_v.at[source],
+            send_sem=b_ss.at[0], recv_sem=b_rs.at[source], device_id={"ctx": nxt}, device_id_type=MESH,
         )
 
     for half in range(2):
@@ -249,37 +249,75 @@
 
         lax.fori_loop(1, 16, send_back, 0)
 
-    def filter_copy(to, source):
-        return pltpu.make_async_remote_copy(
-            src_ref=fsend_v.at[:, pl.ds(pl.multiple_of(to * 32, 32), 32), :], dst_ref=frecv_v.at[source],
-            send_sem=f_ss.at[to], recv_sem=f_rs.at[source], device_id={"dp": to}, device_id_type=MESH,
-        )
-
-    def send_filter(step, carry):
-        filter_copy(lax.rem(dpi + step, 8), dpi).start()
-        return carry
-
-    lax.fori_loop(1, 8, send_filter, 0)
     own_back = pltpu.make_async_copy(
         ysend_v.at[:, pl.ds(pl.multiple_of(me * 16, 16), 16), :], brecv_v.at[me], local_sem.at[1]
     )
     own_back.start()
+    def cross_group(group, carry):
+        spec = spec_v[group].astype(F32)
+        sr, si = spec[:LANES], spec[LANES:]
+        rr, ri = pltpu.roll(sr, HALF, 1), pltpu.roll(si, HALF, 1)
+        cross = ri * sr - rr * si
+        cross = jnp.where(low_lanes(LANES), cross, -cross)
+        freq = jnp.concatenate([sr * rr + si * ri, cross], axis=0).astype(BF16)
+        back = dot(secondt_v[group], freq).astype(BF16).reshape(16, 16, LANES)
+        y_v[:, pl.ds(pl.multiple_of(group * 16, 16), 16), :] = back
+        return carry
+
+    def cross_last(pair, carry):
+        both = jnp.concatenate([y_v[2 * pair], y_v[2 * pair + 1]], axis=1)
+        both = dot(firstt_v[...], both)
+        grad = jnp.where(low_lanes(256), both[:, :LANES], both[:, LANES:]) * scale
+        fsend_v[pair] = grad.astype(BF16)
+        return carry
+
+    lax.fori_loop(0, GROUPS, cross_group, 0, unroll=UNROLL)
+    lax.fori_loop(0, 8, cross_last, 0)
+    row_y, low_x = dpi // 2, lax.rem(dpi, 2)
+
+    def filter_copy(to, source):
+        return pltpu.make_async_remote_copy(
+            src_ref=fsend_v.at[:, pl.ds(pl.multiple_of(to * 64, 64), 64), :], dst_ref=frecv_v.at[source],
+            send_sem=f_ss.at[0], recv_sem=f_rs.at[0], device_id={"dp": 2 * to + low_x}, device_id_type=MESH,
+        )
+
+    for step in range(1, 4):
+        filter_copy(lax.rem(row_y + step, 4), row_y).start()
     own_filter = pltpu.make_async_copy(
-        fsend_v.at[:, pl.ds(pl.multiple_of(dpi * 32, 32), 32), :], frecv_v.at[dpi], local_sem.at[2]
+        fsend_v.at[:, pl.ds(pl.multiple_of(row_y * 64, 64), 64), :], frecv_v.at[row_y], local_sem.at[2]
     )
     own_filter.start()
     own_back.wait()
     own_filter.wait()
+    whole_filter = pltpu.make_async_remote_copy(
+        src_ref=fsend_v.at[:, pl.ds(0, 192), :], dst_ref=frecv_v.at[pl.ds(0, 3)],
+        send_sem=f_ss.at[0], recv_sem=f_rs.at[0], device_id={"dp": dpi}, device_id_type=MESH,
+    )
+    half_filter = pltpu.make_async_remote_copy(
+        src_ref=hsend_v, dst_ref=hrecv_v, send_sem=h_ss.at[0], recv_sem=h_rs.at[0],
+        device_id={"dp": dpi + 1 - 2 * low_x}, device_id_type=MESH,
+    )
+
+    def filter_sum(pair, start):
+        rows = pl.ds(pl.multiple_of(start, 32), 32)
+        value = frecv_v[0, pair, rows, :].astype(F32)
+        for at in range(1, 4):
+            value = value + frecv_v[at, pair, rows, :].astype(F32)
+        return value
+
+    def filter_half(pair, carry):
+        hsend_v[pair] = filter_sum(pair, 32 - 32 * low_x).astype(BF16)
+        return carry
 
     def rim_back_copy(tile, to):
         return pltpu.make_async_remote_copy(
-            src_ref=rsend_v.at[tile], dst_ref=rrecv_v.at[tile], send_sem=r_ss.at[tile], recv_sem=r_rs.at[tile],
+            src_ref=rsend_v.at[tile], dst_ref=rrecv_v.at[tile], send_sem=r_ss.at[0], recv_sem=r_rs.at[0],
             device_id={"ctx": to}, device_id_type=MESH,
         )
 
     def sum_copy(to, source):
         return pltpu.make_async_remote_copy(
-            src_ref=asend_v.at[to], dst_ref=arecv_v.at[source], send_sem=s_ss.at[to], recv_sem=s_rs.at[source],
+            src_ref=asend_v.at[to], dst_ref=arecv_v.at[source], send_sem=s_ss.at[0], recv_sem=s_rs.at[0],
             device_id={"ctx": to}, device_id_type=MESH,
         )
 
@@ -287,14 +325,13 @@
         return jnp.sum(x, axis=0, keepdims=True)
 
     def grad_tile(step, carry):
-        tile = lax.rem(chip + step, 8)
+        tile = lax.rem(chip + 8 - step, 8)
         cols = pl.ds(pl.multiple_of(tile * LANES, LANES), LANES)
         for core in range(2):
 
             @pl.when(2 * tile + core != me)
             def _():
-                back_copy(me, 2 * tile + core, 0).wait_recv()
-                back_copy(me, 2 * tile + core, 1).wait_recv()
+                whole_back(2 * tile + core).wait_recv()
 
         pair = jnp.concatenate(
             [brecv_v[2 * tile].reshape(256, LANES), brecv_v[2 * tile + 1].reshape(256, LANES)], axis=1
@@ -345,79 +382,43 @@
 
     lax.fori_loop(1, 9, grad_tile, 0)
     arecv_v[me] = asend_v[me]
-    stores = [
-        pltpu.make_async_copy(out_v, out_h, store_sem.at[0]),
-        pltpu.make_async_copy(pg_v.at[pl.ds(0, 240)], pg_h.at[pl.ds(0, 240)], store_sem.at[1]),
-    ]
-    for store in stores:
-        store.start()
-
-    def wait_sums(step, carry):
-        sum_copy(me, lax.rem(me + step, 16)).wait_recv()
-        return carry
-
-    lax.fori_loop(1, 16, wait_sums, 0)
+    whole_filter.wait_recv()
+    lax.fori_loop(0, 8, filter_half, 0)
+    half_filter.start()
+    whole_sums = pltpu.make_async_remote_copy(
+        src_ref=asend_v.at[pl.ds(0, 15)], dst_ref=arecv_v.at[pl.ds(0, 15)],
+        send_sem=s_ss.at[0], recv_sem=s_rs.at[0], device_id={"ctx": nxt}, device_id_type=MESH,
+    )
+    whole_sums.wait_recv()
     total = arecv_v[0]
     for at in range(1, 16):
         total = total + arecv_v[at]
-    dsend_v[...] = total
+    dsend_v[...] = jnp.broadcast_to(total[None], dsend_v.shape)
     drecv_v[dpi] = total
 
     def part_copy(to, source):
         return pltpu.make_async_remote_copy(
-            src_ref=dsend_v, dst_ref=drecv_v.at[source], send_sem=d_ss.at[to], recv_sem=d_rs.at[source],
+            src_ref=dsend_v.at[0], dst_ref=drecv_v.at[source], send_sem=d_ss.at[0], recv_sem=d_rs.at[0],
             device_id={"dp": to}, device_id_type=MESH,
         )
 
     def all_copy(to, source):
         return pltpu.make_async_remote_copy(
-            src_ref=gsend_v, dst_ref=grecv_v.at[source], send_sem=g_ss.at[to], recv_sem=g_rs.at[source],
+            src_ref=gsend_v.at[0], dst_ref=grecv_v.at[source], send_sem=g_ss.at[0], recv_sem=g_rs.at[0],
             device_id={"ctx": to}, device_id_type=MESH,
         )
 
-    def send_part(step, carry):
+    for step in range(1, 8):
         part_copy(lax.rem(dpi + step, 8), dpi).start()
-        return carry
-
-    lax.fori_loop(1, 8, send_part, 0)
-
-    def wait_filter(step, carry):
-        filter_copy(dpi, lax.rem(dpi + step, 8)).wait_recv()
-        return carry
-
-    lax.fori_loop(1, 8, wait_filter, 0)
-    for pair in range(8):
-        value = frecv_v[0, pair].astype(F32)
-        for at in range(1, 8):
-            value = value + frecv_v[at, pair].astype(F32)
-        fg_v[pl.ds(2 * pair, 32, 16), :] = value[:, :HALF]
-        fg_v[pl.ds(2 * pair + 1, 32, 16), :] = pltpu.roll(value, HALF, 1)[:, :HALF]
-    store = pltpu.make_async_copy(fg_v, fg_h, store_sem.at[2])
-    store.start()
-    stores.append(store)
-
-    def wait_part(step, carry):
-        part_copy(dpi, lax.rem(dpi + step, 8)).wait_recv()
-        return carry
-
-    lax.fori_loop(1, 8, wait_part, 0)
-    total = drecv_v[0]
-    for at in range(1, 8):
-        total = total + drecv_v[at]
-    total = total * scale
-    gsend_v[...] = total
-    grecv_v[me] = total
-
-    def send_all(step, carry):
-        all_copy(lax.rem(me + step, 16), me).start()
-        return carry
-
-    lax.fori_loop(1, 16, send_all, 0)
 
     keep_back = jnp.where(me == 15, 0.0, 1.0).astype(F32)
+    whole_rims = pltpu.make_async_remote_copy(
+        src_ref=rsend_v, dst_ref=rrecv_v, send_sem=r_ss.at[0], recv_sem=r_rs.at[0],
+        device_id={"ctx": prv}, device_id_type=MESH,
+    )
+    whole_rims.wait_recv()
 
     def fix_tile(tile, carry):
-        rim_back_copy(tile, prv).wait_recv()
         row = lax.broadcasted_iota(jnp.int32, (16, LANES), 0)
         for part in range(3):
             cut = pl.ds(pl.multiple_of(tile * LANES + part * 1024, LANES), LANES)
@@ -430,72 +431,70 @@
         return carry
 
     lax.fori_loop(0, 8, fix_tile, 0)
-    store = pltpu.make_async_copy(pg_v.at[pl.ds(240, 16)], pg_h.at[pl.ds(240, 16)], store_sem.at[3])
-    store.start()
-    stores.append(store)
-
-    def wait_all(step, carry):
-        all_copy(me, lax.rem(me + step, 16)).wait_recv()
-        return carry
-
-    lax.fori_loop(1, 16, wait_all, 0)
+
+    whole_parts = pltpu.make_async_remote_copy(
+        src_ref=dsend_v.at[pl.ds(0, 7)], dst_ref=drecv_v.at[pl.ds(0, 7)],
+        send_sem=d_ss.at[0], recv_sem=d_rs.at[0], device_id={"ctx": nxt}, device_id_type=MESH,
+    )
+    whole_parts.wait_recv()
+    total = drecv_v[0]
+    for at in range(1, 8):
+        total = total + drecv_v[at]
+    total = total * scale
+    gsend_v[0] = total
+    grecv_v[me] = total
+    for step in range(1, 16):
+        all_copy(lax.rem(me + step, 16), me).start()
+
+    half_filter.wait_recv()
+    for pair in range(8):
+        value = filter_sum(pair, 32 * low_x) + hrecv_v[pair].astype(F32)
+        wide_v[pl.ds(2 * pair, 32, 16), :] = value
+        wide_v[pl.ds(2 * pair + 1, 32, 16), :] = pltpu.roll(value, HALF, 1)
+    fg_v[...] = jnp.transpose(wide_v[...])[:HALF]
+
+    whole_forward.wait_send()
+    whole_back(me).wait_send()
+    whole_filter.wait_send()
+    half_filter.wait_send()
+    whole_rims.wait_send()
+    whole_sums.wait_send()
+    whole_parts.wait_send()
+    whole_all = pltpu.make_async_remote_copy(
+        src_ref=gsend_v.at[pl.ds(0, 15)], dst_ref=grecv_v.at[pl.ds(0, 15)],
+        send_sem=g_ss.at[0], recv_sem=g_rs.at[0], device_id={"ctx": nxt}, device_id_type=MESH,
+    )
+    whole_all.wait_recv()
     for tile in range(8):
         for at in range(9):
             part, tap = at // 3, at % 3
             left = part * 1024 + tile * LANES
             sg_v[tap : tap + 1, left : left + LANES] = grecv_v[2 * tile + at // 8, at % 8 : at % 8 + 1]
         skg_v[:, tile * LANES : tile * LANES + LANES] = grecv_v[2 * tile + 1, 1:2]
-    for at, (src, dst) in enumerate([(sg_v, sg_h), (skg_v, skg_h)]):
-        store = pltpu.make_async_copy(src, dst, store_sem.at[4 + at])
-        store.start()
-        stores.append(store)
-
-    def wait_sends(step, carry):
-        to = lax.rem(me + step, 16)
-        forward_copy(to, me).wait_send()
-        back_copy(to, me, 0).wait_send()
-        back_copy(to, me, 1).wait_send()
-        sum_copy(to, me).wait_send()
-        all_copy(to, me).wait_send()
-        return carry
-
-    def wait_dp_sends(step, carry):
-        to = lax.rem(dpi + step, 8)
-        filter_copy(to, dpi).wait_send()
-        part_copy(to, dpi).wait_send()
-        return carry
-
-    def wait_rim_sends(tile, carry):
-        rim_back_copy(tile, prv).wait_send()
-        return carry
-
-    lax.fori_loop(1, 16, wait_sends, 0)
-    lax.fori_loop(1, 8, wait_dp_sends, 0)
-    lax.fori_loop(0, 8, wait_rim_sends, 0)
-    for store in stores:
-        store.wait()
+    whole_all.wait_send()
 
 
 def shards(proj, short_w, filt, skip_gain, cotangent):
     width = skip_gain.shape[0]
     scale = 1.0 / math.sqrt(proj.shape[0] * lax.axis_size("dp") * lax.axis_size("ctx"))
     whole = pl.BlockSpec(memory_space=pl.ANY)
+    inside = pl.BlockSpec(memory_space=pltpu.VMEM)
     dma = pltpu.SemaphoreType.DMA
     outs = pl.pallas_call(
         functools.partial(kernel, scale),
         out_shape=[
-            jax.ShapeDtypeStruct((256, 1024), BF16),
-            jax.ShapeDtypeStruct((256, 3072), BF16),
-            jax.ShapeDtypeStruct((3, 3072), F32),
-            jax.ShapeDtypeStruct((1, 1024), F32),
-            jax.ShapeDtypeStruct((512, HALF), F32),
+            pltpu.VMEM((256, 1024), BF16),
+            pltpu.VMEM((256, 3072), BF16),
+            pltpu.VMEM((3, 3072), F32),
+            pltpu.VMEM((1, 1024), F32),
+            pltpu.VMEM((HALF, 512), F32),
         ],
         in_specs=[whole] * 11,
-        out_specs=[whole] * 5,
+        out_specs=[inside] * 5,
         scratch_shapes=[
             pltpu.VMEM((256, 3072), BF16),
             pltpu.VMEM((256, 1024), BF16),
-            pltpu.VMEM((4096, HALF), F32),
+            pltpu.VMEM((HALF, 4096), F32),
             pltpu.VMEM((3, 3072), F32),
             pltpu.VMEM((1, 1024), F32),
             pltpu.VMEM((256, 256), BF16),
@@ -511,36 +510,35 @@
             pltpu.VMEM((LO, HI, LANES), BF16),
             pltpu.VMEM((LO, 2 * HI, LANES), BF16),
             pltpu.VMEM((GROUPS, 256, LANES), F32),
-            pltpu.VMEM((LO, 2 * HI, 2 * LANES), BF16),
+            pltpu.VMEM((GROUPS, 256, LANES), BF16),
+            pltpu.VMEM((LO, 2 * HI, LANES), BF16),
             pltpu.VMEM((LO, HI, LANES), BF16),
             pltpu.VMEM((16, LO, 16, LANES), BF16),
             pltpu.VMEM((8, HI, LANES), BF16),
-            pltpu.VMEM((8, 8, 32, LANES), BF16),
-            pltpu.VMEM((256, 1024), BF16),
-            pltpu.VMEM((256, 3072), BF16),
+            pltpu.VMEM((4, 8, 64, LANES), BF16),
+            pltpu.VMEM((8, 32, LANES), BF16),
+            pltpu.VMEM((8, 32, LANES), BF16),
             pltpu.VMEM((8, 48, LANES), F32),
             pltpu.VMEM((8, 48, LANES), BF16),
             pltpu.VMEM((8, 48, LANES), BF16),
             pltpu.VMEM((16, 8, LANES), F32),
             pltpu.VMEM((16, 8, LANES), F32),
-            pltpu.VMEM((8, LANES), F32),
             pltpu.VMEM((8, 8, LANES), F32),
-            pltpu.VMEM((8, LANES), F32),
+            pltpu.VMEM((8, 8, LANES), F32),
             pltpu.VMEM((16, 8, LANES), F32),
-            pltpu.VMEM((3, 3072), F32),
-            pltpu.VMEM((1, 1024), F32),
-            pltpu.VMEM((512, HALF), F32),
+            pltpu.VMEM((16, 8, LANES), F32),
+            pltpu.VMEM((512, LANES), F32),
             dma((11,)),
-            dma((1,)), dma((1,)), dma((16,)), dma((16,)), dma((2, 16)), dma((2, 16)), dma((8,)), dma((8,)),
-            dma((8,)), dma((8,)), dma((16,)), dma((16,)), dma((8,)), dma((8,)), dma((16,)), dma((16,)),
-            dma((3,)), dma((6,)),
+            dma((1,)), dma((1,)), dma((1,)), dma((1,)), dma((1,)), dma((16,)), dma((1,)), dma((1,)),
+            dma((1,)), dma((1,)), dma((1,)), dma((1,)), dma((1,)), dma((1,)), dma((1,)), dma((1,)),
+            dma((1,)), dma((1,)), dma((3,)),
         ],
         compiler_params=pltpu.CompilerParams(
             collective_id=0, has_side_effects=True, vmem_limit_bytes=56 * 1024 * 1024
         ),
-    )(proj, cotangent, filt, short_w, skip_gain.reshape(1, width), *tables())
+    )(proj, cotangent, filt.T, short_w, skip_gain.reshape(1, width), *tables())
     outputs, proj_grad, short_grad, skip_grad, filt_grad = outs
-    return (outputs, proj_grad, short_grad, skip_grad.reshape(width), filt_grad)
+    return (outputs, proj_grad, short_grad, skip_grad.reshape(width), filt_grad.T)
 
 
 def solution(mesh):

time: 91.1 us -> 69.2 us (0.76)
  Pallas kernels: 79.6 us -> 64.6 us
  local copies, waits for them, and re-layouts: 10.6 us -> 3.81 us
    pallas_call x1, Pallas kernels: 79.6 us -> 64.6 us  [shards(): pl.pallas_call(functools.partial(kernel, scale), out_shape=[pltpu.VMEM((2...]
    unnamed x10 -> x5, local copies, waits for them, and re-layouts: 10.6 us -> 3.81 us
where the time goes in v1:
time: 69.2 us; the launch traced here: 69.1 us
  Pallas kernels  64.6 us (93%)
  local copies, waits for them, and re-layouts  3.81 us (6%)
    pallas_call x1, Pallas kernels, shards(): pl.pallas_call(functools.partial(kernel, scale), out_shape=[pltpu.VMEM((2...  64.6 us
    unnamed x5, local copies, waits for them, and re-layouts  3.81 us

profile of v1, /device:TPU:1, one launch (start us, length us, event | category | flops | bytes accessed | tf_op | source)
XLA Modules:
  0.0 69.1 jit_solution(15592123526773326030)
XLA Ops:
  0.6 64.6 %shard_map.146 = (bf16[256,1024]{1,0:T(8,128)(2,1)S(1)}, bf16[256,3072]{1,0:T(8,128)(2,1)S(1)}, f32[3,3072]{1,0:T(4,128)S(1)}, f32[1,1024]{1,0:T(1,128)S(1)}, f32[64,512]{1,0:T(8,128)S(1)}) custom-call(bf16[256,3072]{1,0:T(8,128)(2,1)} %proj_h.1, bf16[256,1024]{1,0:T(8,128)(2,1)} %cot_h.1, f32[64,4096]{1,0:T(8,128)} %bitcast.6, f32[3,3072]{1,0:T(4,128)} %short_h.1, ...), custom_call_target="tpu_custom_call" | custom-call | tf_op jit(solution)/shard_map/pallas_call | solution.py:483
  65.3 0.8 %copy.21 = bf16[256,1024]{1,0:T(8,128)(2,1)} copy(bf16[256,1024]{1,0:T(8,128)(2,1)S(1)} %get-tuple-element.15) | data formatting | bytes 1048576
  66.1 0.6 copy.24
  66.7 0.6 copy.23
  67.3 0.7 copy.25
  67.9 1.1 %copy.22 = bf16[256,3072]{1,0:T(8,128)(2,1)} copy(bf16[256,3072]{1,0:T(8,128)(2,1)S(1)} %get-tuple-element.16) | data formatting | bytes 3145728

commit v2 on v1

--- a/solution.py
+++ b/solution.py
@@ -15,6 +15,9 @@
 GROUP = 8
 GROUPS = HI // GROUP
 UNROLL = 4
+U1 = 8
+U2 = 4
+U3 = 16
 LANES = 128
 HALF = 64
 MESH = pl.DeviceIdType.MESH
@@ -61,22 +64,23 @@
     return jnp.concatenate([jnp.where(row < steps, before, turned[:8]), turned[8:]], axis=0)
 
 
-def advanced(x, steps):
+def advanced(x, rim, steps):
     rows = x.shape[0]
     turned = pltpu.roll(x, rows - steps, 0)
+    after = pltpu.roll(rim, 8 - steps, 0)
     row = lax.broadcasted_iota(jnp.int32, (8, LANES), 0)
     return jnp.concatenate(
-        [turned[: rows - 8], jnp.where(row < 8 - steps, turned[rows - 8 :], 0.0)], axis=0
+        [turned[: rows - 8], jnp.where(row < 8 - steps, turned[rows - 8 :], after)], axis=0
     )
 
 
 def kernel(
     scale,
     proj_h, cot_h, filt_h, short_h, skip_h, perm_h, unperm_h, first_h, second_h, firstt_h, secondt_h,
-    out_v, pg_v, sg_v, skg_v, fg_v,
+    out_v, pg_v, grecv_v, fg_v,
     proj_v, cot_v, filt_v, short_v, skip_v, perm_v, unperm_v, first_v, second_v, firstt_v, secondt_v,
     rim_v, mix_v, send_v, recv_v, fx_v, y_v, fs_v, spec_v, z_v, ysend_v, brecv_v, fsend_v, frecv_v, hsend_v, hrecv_v,
-    tail_v, rsend_v, rrecv_v, asend_v, arecv_v, dsend_v, drecv_v, gsend_v, grecv_v, wide_v,
+    xs_v, ready_v, mg_v, rsend_v, rrecv_v, asend_v, arecv_v, dsend_v, drecv_v, gsend_v, wide_v,
     load_sem, rim_ss, rim_rs, a_ss, a_rs, b_ss, b_rs, f_ss, f_rs, h_ss, h_rs, r_ss, r_rs, s_ss, s_rs, d_ss, d_rs,
     g_ss, g_rs, local_sem,
 ):
@@ -106,7 +110,7 @@
             ]
         )
     ]
-    for load in loads:
+    for load in loads[:4]:
         load.start()
     asend_v[...] = jnp.zeros_like(asend_v)
     pl.semaphore_wait(barrier, 22)
@@ -120,12 +124,14 @@
     rim_copy(nxt).start()
     for load in loads[:4]:
         load.wait()
-    rim_copy(nxt).wait()
+    for load in loads[4:]:
+        load.start()
     keep = jnp.where(me == 0, 0.0, 1.0).astype(F32)
 
-    def forward_copy(to, source):
-        return pltpu.make_async_remote_copy(
-            src_ref=send_v.at[to], dst_ref=recv_v.at[:, pl.ds(pl.multiple_of(source * 16, 16), 16), :],
+    def forward_copy(to, source, start, count):
+        return pltpu.make_async_remote_copy(
+            src_ref=send_v.at[to, pl.ds(start, count)],
+            dst_ref=recv_v.at[pl.ds(start, count), pl.ds(pl.multiple_of(source * 16, 16), 16), :],
             send_sem=a_ss.at[0], recv_sem=a_rs.at[0], device_id={"ctx": to}, device_id_type=MESH,
         )
 
@@ -136,9 +142,8 @@
         for part in range(3):
             cut = pl.ds(pl.multiple_of(tile * LANES + part * 1024, LANES), LANES)
             x = proj_v[:, cut].astype(F32)
-            rim = rim_v[:, cut].astype(F32)[8:16] * keep
             w = short_v[:, cut]
-            value = w[0:1] * x + w[1:2] * delayed(x, rim, 1) + w[2:3] * delayed(x, rim, 2)
+            value = w[0:1] * x + w[1:2] * pltpu.roll(x, 1, 0) + w[2:3] * pltpu.roll(x, 2, 0)
             mix_v[part, :, cols] = value
             mixed.append(value)
         product = (mixed[1] * mixed[2]).astype(BF16)
@@ -154,11 +159,43 @@
 
             @pl.when(2 * tile + core != me)
             def _():
-                forward_copy(2 * tile + core, me).start()
+                forward_copy(2 * tile + core, me, 2, 14).start()
+
+        return carry
+
+    def gate_head(step, carry):
+        tile = lax.rem(chip + step, 8)
+        cols = pl.ds(pl.multiple_of(tile * LANES, LANES), LANES)
+        mixed = []
+        for part in range(3):
+            cut = pl.ds(pl.multiple_of(tile * LANES + part * 1024, LANES), LANES)
+            x = proj_v[pl.ds(0, 16), cut].astype(F32)
+            rim = rim_v[:, cut].astype(F32)[8:16] * keep
+            w = short_v[:, cut]
+            value = (w[0:1] * x + w[1:2] * delayed(x, rim, 1) + w[2:3] * delayed(x, rim, 2))[:8]
+            mix_v[part, pl.ds(0, 8), cols] = value
+            mixed.append(value)
+        p = (mixed[1] * mixed[2]).astype(BF16).astype(F32)
+        g = (cot_v[pl.ds(0, 16), cols].astype(F32)[:8] * mixed[0]).astype(BF16).astype(F32)
+        low = low_lanes(8)
+        row = lax.broadcasted_iota(jnp.int32, (16, LANES), 0)
+        for core, head in enumerate(
+            (jnp.where(low, p, pltpu.roll(g, HALF, 1)), jnp.where(low, pltpu.roll(p, HALF, 1), g))
+        ):
+            for at in range(2):
+                block = send_v[2 * tile + core, at].astype(F32)
+                block = jnp.where(row == 0, head[at : at + 1], block)
+                send_v[2 * tile + core, at] = block.astype(BF16)
+
+            @pl.when(2 * tile + core != me)
+            def _():
+                forward_copy(2 * tile + core, me, 0, 2).start()
 
         return carry
 
     lax.fori_loop(1, 9, gate_tile, 0)
+    rim_copy(nxt).wait()
+    lax.fori_loop(1, 9, gate_head, 0)
     own = pltpu.make_async_copy(
         send_v.at[me], recv_v.at[:, pl.ds(pl.multiple_of(me * 16, 16), 16), :], local_sem.at[0]
     )
@@ -206,11 +243,11 @@
     )
     whole_forward.wait_recv()
 
-    lax.fori_loop(0, 8, functools.partial(first_stage, recv_v), 0)
+    lax.fori_loop(0, 8, functools.partial(first_stage, recv_v), 0, unroll=U1)
 
     def middle_group(group, carry):
         spec = second_stage(group)
-        spec_v[group] = spec.astype(BF16)
+        spec_v[group] = spec
         sr, si = spec[:LANES], spec[LANES:]
         fr, fi = fs_v[group, :LANES], fs_v[group, LANES:]
         freq = jnp.concatenate([sr * fr - si * fi, sr * fi + si * fr], axis=0).astype(BF16)
@@ -218,7 +255,7 @@
         z_v[:, pl.ds(pl.multiple_of(group * 16, 16), 16), :] = back
         return carry
 
-    lax.fori_loop(0, GROUPS, middle_group, 0, unroll=UNROLL)
+    lax.fori_loop(0, GROUPS, middle_group, 0, unroll=U3)
 
     def last_stage(pair, carry):
         both = jnp.concatenate([z_v[2 * pair], z_v[2 * pair + 1]], axis=1)
@@ -241,7 +278,7 @@
         )
 
     for half in range(2):
-        lax.fori_loop(4 * half, 4 * half + 4, last_stage, 0)
+        lax.fori_loop(4 * half, 4 * half + 4, last_stage, 0, unroll=U2)
 
         def send_back(step, carry, half=half):
             back_copy(lax.rem(me + step, 16), me, half).start()
@@ -254,7 +291,7 @@
     )
     own_back.start()
     def cross_group(group, carry):
-        spec = spec_v[group].astype(F32)
+        spec = spec_v[group]
         sr, si = spec[:LANES], spec[LANES:]
         rr, ri = pltpu.roll(sr, HALF, 1), pltpu.roll(si, HALF, 1)
         cross = ri * sr - rr * si
@@ -324,53 +361,59 @@
     def down(x):
         return jnp.sum(x, axis=0, keepdims=True)
 
-    def grad_tile(step, carry):
-        tile = lax.rem(chip + 8 - step, 8)
+    def ready_tile(tile, carry):
         cols = pl.ds(pl.multiple_of(tile * LANES, LANES), LANES)
-        for core in range(2):
-
-            @pl.when(2 * tile + core != me)
-            def _():
-                whole_back(2 * tile + core).wait_recv()
-
-        pair = jnp.concatenate(
-            [brecv_v[2 * tile].reshape(256, LANES), brecv_v[2 * tile + 1].reshape(256, LANES)], axis=1
-        )
-        pair = dot(unperm_v[...], pair)
-        even, odd = pair[:, :LANES], pair[:, LANES:]
-        low = low_lanes(256)
-        long_part = jnp.where(low, even, pltpu.roll(odd, HALF, 1))
-        back_part = jnp.where(low, pltpu.roll(even, HALF, 1), odd)
         queries, keys, values = (mix_v[part, :, cols] for part in range(3))
         cot = cot_v[:, cols].astype(F32)
         gain = skip_v[:, cols]
         product = (keys * values).astype(BF16).astype(F32)
         grad = (cot * queries).astype(BF16).astype(F32)
-        gated = long_part + gain * product
+        ready_v[0, :, cols] = gain * product
+        ready_v[1, :, cols] = gain * grad
+        ready_v[2, :, cols] = cot
+        asend_v[2 * tile + 1, 1:2] = down(grad * product)
+        for part in range(3):
+            cut = pl.ds(pl.multiple_of(tile * LANES + part * 1024, LANES), LANES)
+            x = proj_v[:, cut].astype(F32)
+            rim = rim_v[:, cut].astype(F32)[8:16] * keep
+            xs_v[0, :, cut] = delayed(x, rim, 1)
+            xs_v[1, :, cut] = delayed(x, rim, 2)
+        return carry
+
+    lax.fori_loop(0, 8, ready_tile, 0)
+    whole_filter.wait_recv()
+    lax.fori_loop(0, 8, filter_half, 0)
+    half_filter.start()
+
+    def grad_tile(step, carry):
+        tile = lax.rem(chip + 8 - step, 8)
+        cols = pl.ds(pl.multiple_of(tile * LANES, LANES), LANES)
+        for core in range(2):
+
+            @pl.when(2 * tile + core != me)
+            def _():
+                whole_back(2 * tile + core).wait_recv()
+
+        pair = jnp.concatenate(
+            [brecv_v[2 * tile].reshape(256, LANES), brecv_v[2 * tile + 1].reshape(256, LANES)], axis=1
+        )
+        pair = dot(unperm_v[...], pair)
+        even, odd = pair[:, :LANES], pair[:, LANES:]
+        low = low_lanes(256)
+        gated = jnp.where(low, even, pltpu.roll(odd, HALF, 1)) + ready_v[0, :, cols]
+        product_grad = jnp.where(low, pltpu.roll(even, HALF, 1), odd) + ready_v[1, :, cols]
+        queries, keys, values = (mix_v[part, :, cols] for part in range(3))
         out_v[:, cols] = (queries * gated).astype(BF16)
-        product_grad = back_part + gain * grad
-        for part, mixed_grad in enumerate((cot * gated, product_grad * values, product_grad * keys)):
+        for part, mixed_grad in enumerate((ready_v[2, :, cols] * gated, product_grad * values, product_grad * keys)):
             cut = pl.ds(pl.multiple_of(tile * LANES + part * 1024, LANES), LANES)
             rounded = mixed_grad.astype(BF16)
+            mg_v[:, cut] = rounded
             rsend_v[tile, 16 * part : 16 * part + 16] = rounded[:16]
             mg = rounded.astype(F32)
-            one, two = advanced(mg, 1), advanced(mg, 2)
-            w = short_v[:, cut]
-            value = w[0:1] * mg + w[1:2] * one + w[2:3] * two
-            pg_v[:, cut] = value.astype(BF16)
-            tail_v[tile, 16 * part : 16 * part + 16] = value[240:]
-            x = proj_v[:, cut].astype(F32)
-            rim = rim_v[:, cut].astype(F32)[8:16] * keep
-            head = mg[:8]
-            sums = [
-                down(mg * x),
-                down(one * x) + head[0:1] * rim[7:8],
-                down(two * x) + head[0:1] * rim[6:7] + head[1:2] * rim[7:8],
-            ]
+            sums = [down(mg * x) for x in (proj_v[:, cut].astype(F32), xs_v[0, :, cut], xs_v[1, :, cut])]
             for tap in range(3):
                 at = 3 * part + tap
                 asend_v[2 * tile + at // 8, at % 8 : at % 8 + 1] = sums[tap]
-        asend_v[2 * tile + 1, 1:2] = down(grad * product)
         rim_back_copy(tile, prv).start()
         for core in range(2):
 
@@ -382,9 +425,12 @@
 
     lax.fori_loop(1, 9, grad_tile, 0)
     arecv_v[me] = asend_v[me]
-    whole_filter.wait_recv()
-    lax.fori_loop(0, 8, filter_half, 0)
-    half_filter.start()
+    half_filter.wait_recv()
+    for pair in range(8):
+        value = filter_sum(pair, 32 * low_x) + hrecv_v[pair].astype(F32)
+        wide_v[pl.ds(2 * pair, 32, 16), :] = value
+        wide_v[pl.ds(2 * pair + 1, 32, 16), :] = pltpu.roll(value, HALF, 1)
+    fg_v[...] = jnp.transpose(wide_v[...])[:HALF]
     whole_sums = pltpu.make_async_remote_copy(
         src_ref=asend_v.at[pl.ds(0, 15)], dst_ref=arecv_v.at[pl.ds(0, 15)],
         send_sem=s_ss.at[0], recv_sem=s_rs.at[0], device_id={"ctx": nxt}, device_id_type=MESH,
@@ -418,19 +464,17 @@
     )
     whole_rims.wait_recv()
 
-    def fix_tile(tile, carry):
-        row = lax.broadcasted_iota(jnp.int32, (16, LANES), 0)
+    def last_tile(tile, carry):
         for part in range(3):
             cut = pl.ds(pl.multiple_of(tile * LANES + part * 1024, LANES), LANES)
-            rim = rrecv_v[tile, 16 * part : 16 * part + 16].astype(F32) * keep_back
+            rim = rrecv_v[tile, 16 * part : 16 * part + 16].astype(F32)[:8] * keep_back
+            mg = mg_v[:, cut].astype(F32)
             w = short_v[:, cut]
-            value = tail_v[tile, 16 * part : 16 * part + 16]
-            value = value + jnp.where(row == 15, w[1:2] * rim[0:1] + w[2:3] * rim[1:2], 0.0)
-            value = value + jnp.where(row == 14, w[2:3] * rim[0:1], 0.0)
-            pg_v[pl.ds(240, 16), cut] = value.astype(BF16)
-        return carry
-
-    lax.fori_loop(0, 8, fix_tile, 0)
+            value = w[0:1] * mg + w[1:2] * advanced(mg, rim, 1) + w[2:3] * advanced(mg, rim, 2)
+            pg_v[:, cut] = value.astype(BF16)
+        return carry
+
+    lax.fori_loop(0, 4, last_tile, 0)
 
     whole_parts = pltpu.make_async_remote_copy(
         src_ref=dsend_v.at[pl.ds(0, 7)], dst_ref=drecv_v.at[pl.ds(0, 7)],
@@ -446,13 +490,7 @@
     for step in range(1, 16):
         all_copy(lax.rem(me + step, 16), me).start()
 
-    half_filter.wait_recv()
-    for pair in range(8):
-        value = filter_sum(pair, 32 * low_x) + hrecv_v[pair].astype(F32)
-        wide_v[pl.ds(2 * pair, 32, 16), :] = value
-        wide_v[pl.ds(2 * pair + 1, 32, 16), :] = pltpu.roll(value, HALF, 1)
-    fg_v[...] = jnp.transpose(wide_v[...])[:HALF]
-
+    lax.fori_loop(4, 8, last_tile, 0)
     whole_forward.wait_send()
     whole_back(me).wait_send()
     whole_filter.wait_send()
@@ -465,13 +503,26 @@
         send_sem=g_ss.at[0], recv_sem=g_rs.at[0], device_id={"ctx": nxt}, device_id_type=MESH,
     )
     whole_all.wait_recv()
+    whole_all.wait_send()
+
+
+def result_kernel(out_v, pg_v, sums_v, fg_v, out_r, pg_r, sg_r, skg_r, fg_r, sg_v, skg_v, sem):
+    copies = [
+        pltpu.make_async_copy(src, dst, sem.at[at])
+        for at, (src, dst) in enumerate([(pg_v, pg_r), (out_v, out_r), (fg_v, fg_r), (sg_v, sg_r), (skg_v, skg_r)])
+    ]
+    for copy in copies[:3]:
+        copy.start()
     for tile in range(8):
         for at in range(9):
             part, tap = at // 3, at % 3
             left = part * 1024 + tile * LANES
-            sg_v[tap : tap + 1, left : left + LANES] = grecv_v[2 * tile + at // 8, at % 8 : at % 8 + 1]
-        skg_v[:, tile * LANES : tile * LANES + LANES] = grecv_v[2 * tile + 1, 1:2]
-    whole_all.wait_send()
+            sg_v[tap : tap + 1, left : left + LANES] = sums_v[2 * tile + at // 8, at % 8 : at % 8 + 1]
+        skg_v[:, tile * LANES : tile * LANES + LANES] = sums_v[2 * tile + 1, 1:2]
+    for copy in copies[3:]:
+        copy.start()
+    for copy in copies:
+        copy.wait()
 
 
 def shards(proj, short_w, filt, skip_gain, cotangent):
@@ -485,12 +536,11 @@
         out_shape=[
             pltpu.VMEM((256, 1024), BF16),
             pltpu.VMEM((256, 3072), BF16),
-            pltpu.VMEM((3, 3072), F32),
-            pltpu.VMEM((1, 1024), F32),
+            pltpu.VMEM((16, 8, LANES), F32),
             pltpu.VMEM((HALF, 512), F32),
         ],
         in_specs=[whole] * 11,
-        out_specs=[inside] * 5,
+        out_specs=[inside] * 4,
         scratch_shapes=[
             pltpu.VMEM((256, 3072), BF16),
             pltpu.VMEM((256, 1024), BF16),
@@ -510,7 +560,7 @@
             pltpu.VMEM((LO, HI, LANES), BF16),
             pltpu.VMEM((LO, 2 * HI, LANES), BF16),
             pltpu.VMEM((GROUPS, 256, LANES), F32),
-            pltpu.VMEM((GROUPS, 256, LANES), BF16),
+            pltpu.VMEM((GROUPS, 256, LANES), F32),
             pltpu.VMEM((LO, 2 * HI, LANES), BF16),
             pltpu.VMEM((LO, HI, LANES), BF16),
             pltpu.VMEM((16, LO, 16, LANES), BF16),
@@ -518,14 +568,15 @@
             pltpu.VMEM((4, 8, 64, LANES), BF16),
             pltpu.VMEM((8, 32, LANES), BF16),
             pltpu.VMEM((8, 32, LANES), BF16),
-            pltpu.VMEM((8, 48, LANES), F32),
+            pltpu.VMEM((2, 256, 3072), F32),
+            pltpu.VMEM((3, 256, 1024), F32),
+            pltpu.VMEM((256, 3072), BF16),
             pltpu.VMEM((8, 48, LANES), BF16),
             pltpu.VMEM((8, 48, LANES), BF16),
             pltpu.VMEM((16, 8, LANES), F32),
             pltpu.VMEM((16, 8, LANES), F32),
             pltpu.VMEM((8, 8, LANES), F32),
             pltpu.VMEM((8, 8, LANES), F32),
-            pltpu.VMEM((16, 8, LANES), F32),
             pltpu.VMEM((16, 8, LANES), F32),
             pltpu.VMEM((512, LANES), F32),
             dma((11,)),
@@ -537,7 +588,20 @@
             collective_id=0, has_side_effects=True, vmem_limit_bytes=56 * 1024 * 1024
         ),
     )(proj, cotangent, filt.T, short_w, skip_gain.reshape(1, width), *tables())
-    outputs, proj_grad, short_grad, skip_grad, filt_grad = outs
+    outs = [pltpu.with_memory_space_constraint(value, pltpu.VMEM) for value in outs]
+    outputs, proj_grad, short_grad, skip_grad, filt_grad = pl.pallas_call(
+        result_kernel,
+        out_shape=[
+            jax.ShapeDtypeStruct((256, 1024), BF16),
+            jax.ShapeDtypeStruct((256, 3072), BF16),
+            jax.ShapeDtypeStruct((3, 3072), F32),
+            jax.ShapeDtypeStruct((1, 1024), F32),
+            jax.ShapeDtypeStruct((HALF, 512), F32),
+        ],
+        in_specs=[inside] * 4,
+        out_specs=[whole] * 5,
+        scratch_shapes=[pltpu.VMEM((3, 3072), F32), pltpu.VMEM((1, 1024), F32), dma((5,))],
+    )(*outs)
     return (outputs, proj_grad, short_grad, skip_grad.reshape(width), filt_grad.T)
 
 

time: 69.2 us -> 62.9 us (0.909)
  local copies, waits for them, and re-layouts: 3.81 us -> 0 us
  Pallas kernels: 64.6 us -> 62.1 us
    pallas_call x1, Pallas kernels: 64.6 us -> 60.7 us  [shards(): pl.pallas_call(functools.partial(kernel, scale), out_shape=[pltpu.VMEM((2...]
    unnamed x5 -> x0, local copies, waits for them, and re-layouts: 3.81 us -> none
    pallas_call x0 -> x1, Pallas kernels: none -> 1.4 us  [shards(): pl.pallas_call(result_kernel, out_shape=[jax.ShapeDtypeStruct((256, 1024)...]
where the time goes in v2:
time: 62.9 us; the launch traced here: 62.7 us
  Pallas kernels  62.1 us (99%)
  between operations  0.64 us (1%)
    pallas_call x1, Pallas kernels, shards(): pl.pallas_call(functools.partial(kernel, scale), out_shape=[pltpu.VMEM((2...  60.7 us
    pallas_call x1, Pallas kernels, shards(): pl.pallas_call(result_kernel, out_shape=[jax.ShapeDtypeStruct((256, 1024)...  1.4 us

profile of v2, /device:TPU:1, one launch (start us, length us, event | category | flops | bytes accessed | tf_op | source)
XLA Modules:
  0.0 62.7 jit_solution(16915898011050365255)
XLA Ops:
  0.6 60.7 %shard_map.146 = (bf16[256,1024]{1,0:T(8,128)(2,1)S(1)}, bf16[256,3072]{1,0:T(8,128)(2,1)S(1)}, f32[16,8,128]{2,1,0:T(8,128)S(1)}, f32[64,512]{1,0:T(8,128)S(1)}) custom-call(bf16[256,3072]{1,0:T(8,128)(2,1)} %proj_h.1, bf16[256,1024]{1,0:T(8,128)(2,1)} %cot_h.1, f32[64,4096]{1,0:T(8,128)} %bitcast.4, f32[3,3072]{1,0:T(4,128)} %short_h.1, ...), custom_call_target="tpu_custom_call" | custom-call | tf_op jit(solution)/shard_map/pallas_call | solution.py:534
  61.3 1.4 %shard_map.147 = (bf16[256,1024]{1,0:T(8,128)(2,1)}, bf16[256,3072]{1,0:T(8,128)(2,1)}, f32[3,3072]{1,0:T(4,128)}, f32[1,1024]{1,0:T(1,128)}, f32[64,512]{1,0:T(8,128)}) custom-call(bf16[256,1024]{1,0:T(8,128)(2,1)S(1)} %get-tuple-element.14.out_v, bf16[256,3072]{1,0:T(8,128)(2,1)S(1)} %get-tuple-element.15.pg_v, ...), custom_call_target="tpu_custom_call" | custom-call | tf_op jit(solution)/shard_map/pallas_call | solution.py:592

commit v3 on v2

--- a/solution.py
+++ b/solution.py
@@ -18,6 +18,7 @@
 U1 = 8
 U2 = 4
 U3 = 16
+CHUNK = 32
 LANES = 128
 HALF = 64
 MESH = pl.DeviceIdType.MESH
@@ -80,7 +81,7 @@
     out_v, pg_v, grecv_v, fg_v,
     proj_v, cot_v, filt_v, short_v, skip_v, perm_v, unperm_v, first_v, second_v, firstt_v, secondt_v,
     rim_v, mix_v, send_v, recv_v, fx_v, y_v, fs_v, spec_v, z_v, ysend_v, brecv_v, fsend_v, frecv_v, hsend_v, hrecv_v,
-    xs_v, ready_v, mg_v, rsend_v, rrecv_v, asend_v, arecv_v, dsend_v, drecv_v, gsend_v, wide_v,
+    xs_v, ready_v, mg_v, gates_v, pair_v, rsend_v, rrecv_v, asend_v, arecv_v, dsend_v, drecv_v, gsend_v, wide_v,
     load_sem, rim_ss, rim_rs, a_ss, a_rs, b_ss, b_rs, f_ss, f_rs, h_ss, h_rs, r_ss, r_rs, s_ss, s_rs, d_ss, d_rs,
     g_ss, g_rs, local_sem,
 ):
@@ -95,9 +96,16 @@
         pl.semaphore_signal(
             barrier, inc=1, device_id={"ctx": lax.rem(me + step, 16)}, device_id_type=MESH
         )
-    for step in range(1, 8):
+    side, seat = me // 8, lax.rem(me, 8)
+    line = side * 8 + dpi
+
+    def line_id(at):
+        return {"dp": lax.rem(at, 8), "ctx": at // 8 * 8 + seat}
+
+    for step in (1, 2, 3, 4, 5, 6, 7, 9, 10, 11, 12, 13, 14, 15):
         pl.semaphore_signal(
-            barrier, inc=1, device_id={"dp": lax.rem(dpi + step, 8)}, device_id_type=MESH
+            barrier, inc=1, device_id=line_id((side if step < 8 else 1 - side) * 8 +
+            lax.rem(dpi + step, 8)), device_id_type=MESH,
         )
 
     loads = [
@@ -113,7 +121,7 @@
     for load in loads[:4]:
         load.start()
     asend_v[...] = jnp.zeros_like(asend_v)
-    pl.semaphore_wait(barrier, 22)
+    pl.semaphore_wait(barrier, 29)
 
     def rim_copy(to):
         return pltpu.make_async_remote_copy(
@@ -135,20 +143,29 @@
             send_sem=a_ss.at[0], recv_sem=a_rs.at[0], device_id={"ctx": to}, device_id_type=MESH,
         )
 
+    def earlier(cut, top, rim=None):
+        x = proj_v[pl.ds(top, CHUNK), cut].astype(F32)
+        before = proj_v[pl.ds(top - 16, 16), cut].astype(F32)[8:] if top else rim
+        if before is None:
+            before = jnp.zeros((8, LANES), F32)
+        return delayed(x, before, 1), delayed(x, before, 2), x
+
     def gate_tile(step, carry):
         tile = lax.rem(chip + step, 8)
         cols = pl.ds(pl.multiple_of(tile * LANES, LANES), LANES)
-        mixed = []
-        for part in range(3):
-            cut = pl.ds(pl.multiple_of(tile * LANES + part * 1024, LANES), LANES)
-            x = proj_v[:, cut].astype(F32)
-            w = short_v[:, cut]
-            value = w[0:1] * x + w[1:2] * pltpu.roll(x, 1, 0) + w[2:3] * pltpu.roll(x, 2, 0)
-            mix_v[part, :, cols] = value
-            mixed.append(value)
-        product = (mixed[1] * mixed[2]).astype(BF16)
-        grad = (cot_v[:, cols].astype(F32) * mixed[0]).astype(BF16)
-        both = dot(perm_v[...], jnp.concatenate([product, grad], axis=1))
+        for top in range(0, 256, CHUNK):
+            rows = pl.ds(top, CHUNK)
+            mixed = []
+            for part in range(3):
+                cut = pl.ds(pl.multiple_of(tile * LANES + part * 1024, LANES), LANES)
+                one, two, x = earlier(cut, top)
+                w = short_v[:, cut]
+                value = w[0:1] * x + w[1:2] * one + w[2:3] * two
+                mix_v[part, rows, cols] = value
+                mixed.append(value)
+            gates_v[rows, :LANES] = (mixed[1] * mixed[2]).astype(BF16)
+            gates_v[rows, LANES:] = (cot_v[rows, cols].astype(F32) * mixed[0]).astype(BF16)
+        both = dot(perm_v[...], gates_v[...])
         p, g = both[:, :LANES], both[:, LANES:]
         low = low_lanes(256)
         even = jnp.where(low, p, pltpu.roll(g, HALF, 1))
@@ -346,160 +363,169 @@
         hsend_v[pair] = filter_sum(pair, 32 - 32 * low_x).astype(BF16)
         return carry
 
-    def rim_back_copy(tile, to):
-        return pltpu.make_async_remote_copy(
-            src_ref=rsend_v.at[tile], dst_ref=rrecv_v.at[tile], send_sem=r_ss.at[0], recv_sem=r_rs.at[0],
-            device_id={"ctx": to}, device_id_type=MESH,
-        )
-
     def sum_copy(to, source):
         return pltpu.make_async_remote_copy(
             src_ref=asend_v.at[to], dst_ref=arecv_v.at[source], send_sem=s_ss.at[0], recv_sem=s_rs.at[0],
-            device_id={"ctx": to}, device_id_type=MESH,
-        )
+            device_id={"ctx": side * 8 + to}, device_id_type=MESH,
+        )
+
+    def partial(x):
+        return jnp.sum(x.reshape(CHUNK // 8, 8, LANES), axis=0)
 
     def down(x):
         return jnp.sum(x, axis=0, keepdims=True)
 
     def ready_tile(tile, carry):
         cols = pl.ds(pl.multiple_of(tile * LANES, LANES), LANES)
-        queries, keys, values = (mix_v[part, :, cols] for part in range(3))
-        cot = cot_v[:, cols].astype(F32)
         gain = skip_v[:, cols]
-        product = (keys * values).astype(BF16).astype(F32)
-        grad = (cot * queries).astype(BF16).astype(F32)
-        ready_v[0, :, cols] = gain * product
-        ready_v[1, :, cols] = gain * grad
-        ready_v[2, :, cols] = cot
-        asend_v[2 * tile + 1, 1:2] = down(grad * product)
-        for part in range(3):
-            cut = pl.ds(pl.multiple_of(tile * LANES + part * 1024, LANES), LANES)
-            x = proj_v[:, cut].astype(F32)
-            rim = rim_v[:, cut].astype(F32)[8:16] * keep
-            xs_v[0, :, cut] = delayed(x, rim, 1)
-            xs_v[1, :, cut] = delayed(x, rim, 2)
+        total = jnp.zeros((8, LANES), F32)
+        for top in range(0, 256, CHUNK):
+            rows = pl.ds(top, CHUNK)
+            queries, keys, values = (mix_v[part, rows, cols] for part in range(3))
+            cot = cot_v[rows, cols].astype(F32)
+            product = (keys * values).astype(BF16).astype(F32)
+            grad = (cot * queries).astype(BF16).astype(F32)
+            ready_v[0, rows, cols] = gain * product
+            ready_v[1, rows, cols] = gain * grad
+            ready_v[2, rows, cols] = cot
+            total = total + partial(grad * product)
+            for part in range(3):
+                cut = pl.ds(pl.multiple_of(tile * LANES + part * 1024, LANES), LANES)
+                one, two, _ = earlier(cut, top, rim_v[:, cut].astype(F32)[8:16] * keep)
+                xs_v[0, rows, cut] = one
+                xs_v[1, rows, cut] = two
+        asend_v[tile, 9:10] = down(total)
         return carry
 
     lax.fori_loop(0, 8, ready_tile, 0)
+    def grad_tile(step, carry):
+        tile = lax.rem(side * 4 + step, 8)
+        cols = pl.ds(pl.multiple_of(tile * LANES, LANES), LANES)
+        for core in range(2):
+
+            @pl.when(2 * tile + core != me)
+            def _():
+                whole_back(2 * tile + core).wait_recv()
+
+        pair = jnp.concatenate(
+            [brecv_v[2 * tile].reshape(256, LANES), brecv_v[2 * tile + 1].reshape(256, LANES)], axis=1
+        )
+        pair_v[...] = dot(unperm_v[...], pair)
+        totals = [jnp.zeros((8, LANES), F32)] * 9
+        low = low_lanes(CHUNK)
+        for top in range(0, 256, CHUNK):
+            rows = pl.ds(top, CHUNK)
+            even, odd = pair_v[rows, :LANES], pair_v[rows, LANES:]
+            gated = jnp.where(low, even, pltpu.roll(odd, HALF, 1)) + ready_v[0, rows, cols]
+            product_grad = jnp.where(low, pltpu.roll(even, HALF, 1), odd) + ready_v[1, rows, cols]
+            queries, keys, values = (mix_v[part, rows, cols] for part in range(3))
+            out_v[rows, cols] = (queries * gated).astype(BF16)
+            grads = (ready_v[2, rows, cols] * gated, product_grad * values, product_grad * keys)
+            for part, mixed_grad in enumerate(grads):
+                cut = pl.ds(pl.multiple_of(tile * LANES + part * 1024, LANES), LANES)
+                rounded = mixed_grad.astype(BF16)
+                mg_v[rows, cut] = rounded
+                mg = rounded.astype(F32)
+                if top == 0:
+                    rsend_v[tile, 2 * part : 2 * part + 2] = mg[:2]
+                lagged = (proj_v[rows, cut].astype(F32), xs_v[0, rows, cut], xs_v[1, rows, cut])
+                for tap in range(3):
+                    totals[3 * part + tap] = totals[3 * part + tap] + partial(mg * lagged[tap])
+        for at in range(9):
+            asend_v[tile, at : at + 1] = down(totals[at])
+
+        @pl.when(tile != seat)
+        def _():
+            sum_copy(tile, seat).start()
+
+        return carry
+
+    rsend_v[...] = jnp.zeros_like(rsend_v)
+    lax.fori_loop(0, 8, grad_tile, 0)
+    rims = pltpu.make_async_remote_copy(
+        src_ref=rsend_v, dst_ref=rrecv_v, send_sem=r_ss.at[0], recv_sem=r_rs.at[0],
+        device_id={"ctx": prv}, device_id_type=MESH,
+    )
+    rims.start()
+    arecv_v[seat] = asend_v[seat]
     whole_filter.wait_recv()
     lax.fori_loop(0, 8, filter_half, 0)
     half_filter.start()
 
-    def grad_tile(step, carry):
-        tile = lax.rem(chip + 8 - step, 8)
-        cols = pl.ds(pl.multiple_of(tile * LANES, LANES), LANES)
-        for core in range(2):
-
-            @pl.when(2 * tile + core != me)
-            def _():
-                whole_back(2 * tile + core).wait_recv()
-
-        pair = jnp.concatenate(
-            [brecv_v[2 * tile].reshape(256, LANES), brecv_v[2 * tile + 1].reshape(256, LANES)], axis=1
-        )
-        pair = dot(unperm_v[...], pair)
-        even, odd = pair[:, :LANES], pair[:, LANES:]
-        low = low_lanes(256)
-        gated = jnp.where(low, even, pltpu.roll(odd, HALF, 1)) + ready_v[0, :, cols]
-        product_grad = jnp.where(low, pltpu.roll(even, HALF, 1), odd) + ready_v[1, :, cols]
-        queries, keys, values = (mix_v[part, :, cols] for part in range(3))
-        out_v[:, cols] = (queries * gated).astype(BF16)
-        for part, mixed_grad in enumerate((ready_v[2, :, cols] * gated, product_grad * values, product_grad * keys)):
+    whole_sums = pltpu.make_async_remote_copy(
+        src_ref=asend_v.at[pl.ds(0, 7)], dst_ref=arecv_v.at[pl.ds(0, 7)],
+        send_sem=s_ss.at[0], recv_sem=s_rs.at[0], device_id={"ctx": nxt}, device_id_type=MESH,
+    )
+    whole_sums.wait_recv()
+    total = arecv_v[0]
+    for at in range(1, 8):
+        total = total + arecv_v[at]
+    dsend_v[0] = total
+    drecv_v[line] = total
+
+    def part_copy(to, source):
+        return pltpu.make_async_remote_copy(
+            src_ref=dsend_v.at[0], dst_ref=drecv_v.at[source], send_sem=d_ss.at[0], recv_sem=d_rs.at[0],
+            device_id=line_id(to), device_id_type=MESH,
+        )
+
+    def all_copy(to, source):
+        return pltpu.make_async_remote_copy(
+            src_ref=gsend_v.at[0], dst_ref=grecv_v.at[source], send_sem=g_ss.at[0], recv_sem=g_rs.at[0],
+            device_id={"ctx": side * 8 + to}, device_id_type=MESH,
+        )
+
+    for step in range(1, 16):
+        part_copy(lax.rem(line + step, 16), line).start()
+
+    keep_back = jnp.where(me == 15, 0.0, 1.0).astype(F32)
+    rims.wait_recv()
+
+    def last_tile(tile, carry):
+        for part in range(3):
             cut = pl.ds(pl.multiple_of(tile * LANES + part * 1024, LANES), LANES)
-            rounded = mixed_grad.astype(BF16)
-            mg_v[:, cut] = rounded
-            rsend_v[tile, 16 * part : 16 * part + 16] = rounded[:16]
-            mg = rounded.astype(F32)
-            sums = [down(mg * x) for x in (proj_v[:, cut].astype(F32), xs_v[0, :, cut], xs_v[1, :, cut])]
-            for tap in range(3):
-                at = 3 * part + tap
-                asend_v[2 * tile + at // 8, at % 8 : at % 8 + 1] = sums[tap]
-        rim_back_copy(tile, prv).start()
-        for core in range(2):
-
-            @pl.when(2 * tile + core != me)
-            def _():
-                sum_copy(2 * tile + core, me).start()
-
-        return carry
-
-    lax.fori_loop(1, 9, grad_tile, 0)
-    arecv_v[me] = asend_v[me]
+            rim = pltpu.roll(rrecv_v[tile], 8 - 2 * part, 0) if part else rrecv_v[tile]
+            rim = rim * keep_back
+            w = short_v[:, cut]
+            for top in range(0, 256, CHUNK):
+                mg = mg_v[pl.ds(top, CHUNK), cut].astype(F32)
+                after = mg_v[pl.ds(top + CHUNK, 16), cut].astype(F32)[:8] if top + CHUNK < 256 else rim
+                value = w[0:1] * mg + w[1:2] * advanced(mg, after, 1) + w[2:3] * advanced(mg, after, 2)
+                pg_v[pl.ds(top, CHUNK), cut] = value.astype(BF16)
+        return carry
+
+    lax.fori_loop(0, 4, last_tile, 0)
+
+    whole_parts = pltpu.make_async_remote_copy(
+        src_ref=dsend_v.at[pl.ds(0, 15)], dst_ref=drecv_v.at[pl.ds(0, 15)],
+        send_sem=d_ss.at[0], recv_sem=d_rs.at[0], device_id={"ctx": nxt}, device_id_type=MESH,
+    )
+    whole_parts.wait_recv()
+    total = drecv_v[0]
+    for at in range(1, 16):
+        total = total + drecv_v[at]
+    total = total * scale
+    gsend_v[0] = total
+    grecv_v[seat] = total
+    for step in range(1, 8):
+        all_copy(lax.rem(seat + step, 8), seat).start()
+
+    lax.fori_loop(4, 8, last_tile, 0)
     half_filter.wait_recv()
     for pair in range(8):
         value = filter_sum(pair, 32 * low_x) + hrecv_v[pair].astype(F32)
         wide_v[pl.ds(2 * pair, 32, 16), :] = value
         wide_v[pl.ds(2 * pair + 1, 32, 16), :] = pltpu.roll(value, HALF, 1)
     fg_v[...] = jnp.transpose(wide_v[...])[:HALF]
-    whole_sums = pltpu.make_async_remote_copy(
-        src_ref=asend_v.at[pl.ds(0, 15)], dst_ref=arecv_v.at[pl.ds(0, 15)],
-        send_sem=s_ss.at[0], recv_sem=s_rs.at[0], device_id={"ctx": nxt}, device_id_type=MESH,
-    )
-    whole_sums.wait_recv()
-    total = arecv_v[0]
-    for at in range(1, 16):
-        total = total + arecv_v[at]
-    dsend_v[...] = jnp.broadcast_to(total[None], dsend_v.shape)
-    drecv_v[dpi] = total
-
-    def part_copy(to, source):
-        return pltpu.make_async_remote_copy(
-            src_ref=dsend_v.at[0], dst_ref=drecv_v.at[source], send_sem=d_ss.at[0], recv_sem=d_rs.at[0],
-            device_id={"dp": to}, device_id_type=MESH,
-        )
-
-    def all_copy(to, source):
-        return pltpu.make_async_remote_copy(
-            src_ref=gsend_v.at[0], dst_ref=grecv_v.at[source], send_sem=g_ss.at[0], recv_sem=g_rs.at[0],
-            device_id={"ctx": to}, device_id_type=MESH,
-        )
-
-    for step in range(1, 8):
-        part_copy(lax.rem(dpi + step, 8), dpi).start()
-
-    keep_back = jnp.where(me == 15, 0.0, 1.0).astype(F32)
-    whole_rims = pltpu.make_async_remote_copy(
-        src_ref=rsend_v, dst_ref=rrecv_v, send_sem=r_ss.at[0], recv_sem=r_rs.at[0],
-        device_id={"ctx": prv}, device_id_type=MESH,
-    )
-    whole_rims.wait_recv()
-
-    def last_tile(tile, carry):
-        for part in range(3):
-            cut = pl.ds(pl.multiple_of(tile * LANES + part * 1024, LANES), LANES)
-            rim = rrecv_v[tile, 16 * part : 16 * part + 16].astype(F32)[:8] * keep_back
-            mg = mg_v[:, cut].astype(F32)
-            w = short_v[:, cut]
-            value = w[0:1] * mg + w[1:2] * advanced(mg, rim, 1) + w[2:3] * advanced(mg, rim, 2)
-            pg_v[:, cut] = value.astype(BF16)
-        return carry
-
-    lax.fori_loop(0, 4, last_tile, 0)
-
-    whole_parts = pltpu.make_async_remote_copy(
-        src_ref=dsend_v.at[pl.ds(0, 7)], dst_ref=drecv_v.at[pl.ds(0, 7)],
-        send_sem=d_ss.at[0], recv_sem=d_rs.at[0], device_id={"ctx": nxt}, device_id_type=MESH,
-    )
-    whole_parts.wait_recv()
-    total = drecv_v[0]
-    for at in range(1, 8):
-        total = total + drecv_v[at]
-    total = total * scale
-    gsend_v[0] = total
-    grecv_v[me] = total
-    for step in range(1, 16):
-        all_copy(lax.rem(me + step, 16), me).start()
-
-    lax.fori_loop(4, 8, last_tile, 0)
     whole_forward.wait_send()
     whole_back(me).wait_send()
     whole_filter.wait_send()
     half_filter.wait_send()
-    whole_rims.wait_send()
+    rims.wait_send()
     whole_sums.wait_send()
     whole_parts.wait_send()
     whole_all = pltpu.make_async_remote_copy(
-        src_ref=gsend_v.at[pl.ds(0, 15)], dst_ref=grecv_v.at[pl.ds(0, 15)],
+        src_ref=gsend_v.at[pl.ds(0, 7)], dst_ref=grecv_v.at[pl.ds(0, 7)],
         send_sem=g_ss.at[0], recv_sem=g_rs.at[0], device_id={"ctx": nxt}, device_id_type=MESH,
     )
     whole_all.wait_recv()
@@ -517,8 +543,8 @@
         for at in range(9):
             part, tap = at // 3, at % 3
             left = part * 1024 + tile * LANES
-            sg_v[tap : tap + 1, left : left + LANES] = sums_v[2 * tile + at // 8, at % 8 : at % 8 + 1]
-        skg_v[:, tile * LANES : tile * LANES + LANES] = sums_v[2 * tile + 1, 1:2]
+            sg_v[tap : tap + 1, left : left + LANES] = sums_v[tile, at : at + 1]
+        skg_v[:, tile * LANES : tile * LANES + LANES] = sums_v[tile, 9:10]
     for copy in copies[3:]:
         copy.start()
     for copy in copies:
@@ -536,7 +562,7 @@
         out_shape=[
             pltpu.VMEM((256, 1024), BF16),
             pltpu.VMEM((256, 3072), BF16),
-            pltpu.VMEM((16, 8, LANES), F32),
+            pltpu.VMEM((8, 16, LANES), F32),
             pltpu.VMEM((HALF, 512), F32),
         ],
         in_specs=[whole] * 11,
@@ -571,13 +597,15 @@
             pltpu.VMEM((2, 256, 3072), F32),
             pltpu.VMEM((3, 256, 1024), F32),
             pltpu.VMEM((256, 3072), BF16),
-            pltpu.VMEM((8, 48, LANES), BF16),
-            pltpu.VMEM((8, 48, LANES), BF16),
-            pltpu.VMEM((16, 8, LANES), F32),
-            pltpu.VMEM((16, 8, LANES), F32),
+            pltpu.VMEM((256, 2 * LANES), BF16),
+            pltpu.VMEM((256, 2 * LANES), F32),
             pltpu.VMEM((8, 8, LANES), F32),
             pltpu.VMEM((8, 8, LANES), F32),
-            pltpu.VMEM((16, 8, LANES), F32),
+            pltpu.VMEM((8, 16, LANES), F32),
+            pltpu.VMEM((8, 16, LANES), F32),
+            pltpu.VMEM((16, 16, LANES), F32),
+            pltpu.VMEM((16, 16, LANES), F32),
+            pltpu.VMEM((8, 16, LANES), F32),
             pltpu.VMEM((512, LANES), F32),
             dma((11,)),
             dma((1,)), dma((1,)), dma((1,)), dma((1,)), dma((1,)), dma((16,)), dma((1,)), dma((1,)),

time: 62.9 us -> 61.6 us (0.979)
  Pallas kernels: 62.1 us -> 60.8 us
    pallas_call x1, Pallas kernels: 60.7 us -> 59.4 us  [shards(): pl.pallas_call(functools.partial(kernel, scale), out_shape=[pltpu.VMEM((2...]
where the time goes in v3:
time: 61.6 us; the launch traced here: 61.5 us
  Pallas kernels  60.8 us (99%)
  between operations  0.64 us (1%)
    pallas_call x1, Pallas kernels, shards(): pl.pallas_call(functools.partial(kernel, scale), out_shape=[pltpu.VMEM((2...  59.4 us
    pallas_call x1, Pallas kernels, shards(): pl.pallas_call(result_kernel, out_shape=[jax.ShapeDtypeStruct((256, 1024)...  1.4 us

profile of v3, /device:TPU:1, one launch (start us, length us, event | category | flops | bytes accessed | tf_op | source)
XLA Modules:
  0.0 61.5 jit_solution(2062002719081036162)
XLA Ops:
  0.6 59.4 %shard_map.146 = (bf16[256,1024]{1,0:T(8,128)(2,1)S(1)}, bf16[256,3072]{1,0:T(8,128)(2,1)S(1)}, f32[8,16,128]{2,1,0:T(8,128)S(1)}, f32[64,512]{1,0:T(8,128)S(1)}) custom-call(bf16[256,3072]{1,0:T(8,128)(2,1)} %proj_h.1, bf16[256,1024]{1,0:T(8,128)(2,1)} %cot_h.1, f32[64,4096]{1,0:T(8,128)} %bitcast.4, f32[3,3072]{1,0:T(4,128)} %short_h.1, ...), custom_call_target="tpu_custom_call" | custom-call | tf_op jit(solution)/shard_map/pallas_call | solution.py:560
  60.1 1.4 %shard_map.147 = (bf16[256,1024]{1,0:T(8,128)(2,1)}, bf16[256,3072]{1,0:T(8,128)(2,1)}, f32[3,3072]{1,0:T(4,128)}, f32[1,1024]{1,0:T(1,128)}, f32[64,512]{1,0:T(8,128)}) custom-call(bf16[256,1024]{1,0:T(8,128)(2,1)S(1)} %get-tuple-element.14.out_v, bf16[256,3072]{1,0:T(8,128)(2,1)S(1)} %get-tuple-element.15.pg_v, ...), custom_call_target="tpu_custom_call" | custom-call | tf_op jit(solution)/shard_map/pallas_call | solution.py:620

commit v4 on v3

--- a/solution.py
+++ b/solution.py
@@ -16,8 +16,8 @@
 GROUPS = HI // GROUP
 UNROLL = 4
 U1 = 8
-U2 = 4
-U3 = 16
+PIECES = 4
+U3 = 32
 CHUNK = 32
 LANES = 128
 HALF = 64
@@ -82,12 +82,13 @@
     proj_v, cot_v, filt_v, short_v, skip_v, perm_v, unperm_v, first_v, second_v, firstt_v, secondt_v,
     rim_v, mix_v, send_v, recv_v, fx_v, y_v, fs_v, spec_v, z_v, ysend_v, brecv_v, fsend_v, frecv_v, hsend_v, hrecv_v,
     xs_v, ready_v, mg_v, gates_v, pair_v, rsend_v, rrecv_v, asend_v, arecv_v, dsend_v, drecv_v, gsend_v, wide_v,
-    load_sem, rim_ss, rim_rs, a_ss, a_rs, b_ss, b_rs, f_ss, f_rs, h_ss, h_rs, r_ss, r_rs, s_ss, s_rs, d_ss, d_rs,
+    load_sem, half_sem, rim_ss, rim_rs, a_ss, a_rs, b_ss, b_rs, f_ss, f_rs, h_ss, h_rs, r_ss, r_rs, s_ss, s_rs, d_ss, d_rs,
     g_ss, g_rs, local_sem,
 ):
     me = lax.axis_index("ctx")
     dpi = lax.axis_index("dp")
-    chip = me // 2
+    side, seat = me // 8, lax.rem(me, 8)
+    level = seat // 2
     nxt = lax.rem(me + 1, 16)
     prv = lax.rem(me + 15, 16)
 
@@ -96,7 +97,6 @@
         pl.semaphore_signal(
             barrier, inc=1, device_id={"ctx": lax.rem(me + step, 16)}, device_id_type=MESH
         )
-    side, seat = me // 8, lax.rem(me, 8)
     line = side * 8 + dpi
 
     def line_id(at):
@@ -112,14 +112,26 @@
         pltpu.make_async_copy(src, dst, load_sem.at[at])
         for at, (src, dst) in enumerate(
             [
-                (proj_h, proj_v), (cot_h, cot_v), (short_h, short_v), (perm_h, perm_v), (filt_h, filt_v),
+                (short_h, short_v), (perm_h, perm_v), (filt_h, filt_v),
                 (first_h, first_v), (second_h, second_v), (secondt_h, secondt_v), (firstt_h, firstt_v),
                 (unperm_h, unperm_v), (skip_h, skip_v),
             ]
         )
     ]
-    for load in loads[:4]:
-        load.start()
+    def half_loads(which):
+        copies = []
+        for part in range(4):
+            cut = pl.ds(pl.multiple_of(which * 512 + part % 3 * 1024, 512), 512)
+            src, dst = (proj_h, proj_v) if part < 3 else (cot_h, cot_v)
+            copies.append(pltpu.make_async_copy(src.at[:, cut], dst.at[:, cut], half_sem.at[part, which]))
+        return copies
+
+    def half_wait(which):
+        for copy in half_loads(which):
+            copy.wait()
+
+    for copy in half_loads(1 - side) + loads[:2] + half_loads(side):
+        copy.start()
     asend_v[...] = jnp.zeros_like(asend_v)
     pl.semaphore_wait(barrier, 29)
 
@@ -130,10 +142,9 @@
         )
 
     rim_copy(nxt).start()
-    for load in loads[:4]:
+    half_wait(1 - side)
+    for load in loads[:2]:
         load.wait()
-    for load in loads[4:]:
-        load.start()
     keep = jnp.where(me == 0, 0.0, 1.0).astype(F32)
 
     def forward_copy(to, source, start, count):
@@ -150,8 +161,12 @@
             before = jnp.zeros((8, LANES), F32)
         return delayed(x, before, 1), delayed(x, before, 2), x
 
+    def far_first(step):
+        across = 1 - step // 4
+        return lax.rem(side + across, 2) * 4 + lax.rem(level + step + 1, 4)
+
     def gate_tile(step, carry):
-        tile = lax.rem(chip + step, 8)
+        tile = far_first(step)
         cols = pl.ds(pl.multiple_of(tile * LANES, LANES), LANES)
         for top in range(0, 256, CHUNK):
             rows = pl.ds(top, CHUNK)
@@ -181,7 +196,7 @@
         return carry
 
     def gate_head(step, carry):
-        tile = lax.rem(chip + step, 8)
+        tile = far_first(step)
         cols = pl.ds(pl.multiple_of(tile * LANES, LANES), LANES)
         mixed = []
         for part in range(3):
@@ -210,9 +225,13 @@
 
         return carry
 
-    lax.fori_loop(1, 9, gate_tile, 0)
+    lax.fori_loop(0, 4, gate_tile, 0)
+    half_wait(side)
+    lax.fori_loop(4, 8, gate_tile, 0)
+    for load in loads[2:]:
+        load.start()
     rim_copy(nxt).wait()
-    lax.fori_loop(1, 9, gate_head, 0)
+    lax.fori_loop(0, 8, gate_head, 0)
     own = pltpu.make_async_copy(
         send_v.at[me], recv_v.at[:, pl.ds(pl.multiple_of(me * 16, 16), 16), :], local_sem.at[0]
     )
@@ -229,7 +248,7 @@
         rows = y_v[:, pl.ds(pl.multiple_of(group * 16, 16), 16), :].reshape(256, LANES)
         return dot(second_v[group], rows)
 
-    for load in loads[4:7]:
+    for load in loads[2:5]:
         load.wait()
 
     def filter_rows(block, carry):
@@ -249,7 +268,7 @@
     lax.fori_loop(0, 16, filter_rows, 0)
     lax.fori_loop(0, 8, functools.partial(first_stage, fx_v), 0)
     lax.fori_loop(0, GROUPS, filter_group, 0, unroll=UNROLL)
-    for load in loads[7:]:
+    for load in loads[5:]:
         load.wait()
 
     own.wait()
@@ -281,10 +300,12 @@
         ysend_v[2 * pair + 1] = both[:, LANES:]
         return carry
 
+    piece = LO // PIECES
+
     def back_copy(to, source, half):
         return pltpu.make_async_remote_copy(
-            src_ref=ysend_v.at[pl.ds(half * 8, 8), pl.ds(pl.multiple_of(to * 16, 16), 16), :],
-            dst_ref=brecv_v.at[source, pl.ds(half * 8, 8)],
+            src_ref=ysend_v.at[pl.ds(half * piece, piece), pl.ds(pl.multiple_of(to * 16, 16), 16), :],
+            dst_ref=brecv_v.at[source, pl.ds(half * piece, piece)],
             send_sem=b_ss.at[0], recv_sem=b_rs.at[source], device_id={"ctx": to}, device_id_type=MESH,
         )
 
@@ -294,14 +315,15 @@
             send_sem=b_ss.at[0], recv_sem=b_rs.at[source], device_id={"ctx": nxt}, device_id_type=MESH,
         )
 
-    for half in range(2):
-        lax.fori_loop(4 * half, 4 * half + 4, last_stage, 0, unroll=U2)
+    for half in range(PIECES):
+        lax.fori_loop(8 // PIECES * half, 8 // PIECES * (half + 1), last_stage, 0, unroll=8 // PIECES)
 
         def send_back(step, carry, half=half):
-            back_copy(lax.rem(me + step, 16), me, half).start()
+            to = lax.rem(side + 1 - step // 8, 2) * 8 + lax.rem(seat + step + 1, 8)
+            back_copy(to, me, half).start()
             return carry
 
-        lax.fori_loop(1, 16, send_back, 0)
+        lax.fori_loop(0, 15, send_back, 0)
 
     own_back = pltpu.make_async_copy(
         ysend_v.at[:, pl.ds(pl.multiple_of(me * 16, 16), 16), :], brecv_v.at[me], local_sem.at[1]
@@ -607,7 +629,7 @@
             pltpu.VMEM((16, 16, LANES), F32),
             pltpu.VMEM((8, 16, LANES), F32),
             pltpu.VMEM((512, LANES), F32),
-            dma((11,)),
+            dma((9,)), dma((4, 2)),
             dma((1,)), dma((1,)), dma((1,)), dma((1,)), dma((1,)), dma((16,)), dma((1,)), dma((1,)),
             dma((1,)), dma((1,)), dma((1,)), dma((1,)), dma((1,)), dma((1,)), dma((1,)), dma((1,)),
             dma((1,)), dma((1,)), dma((3,)),

time: 61.6 us -> 58.9 us (0.956)
  Pallas kernels: 60.8 us -> 58.1 us
    pallas_call x1, Pallas kernels: 59.4 us -> 56.7 us  [shards(): pl.pallas_call(functools.partial(kernel, scale), out_shape=[pltpu.VMEM((2...]
where the time goes in v4:
time: 58.9 us; the launch traced here: 58.7 us
  Pallas kernels  58.1 us (99%)
  between operations  0.64 us (1%)
    pallas_call x1, Pallas kernels, shards(): pl.pallas_call(functools.partial(kernel, scale), out_shape=[pltpu.VMEM((2...  56.7 us
    pallas_call x1, Pallas kernels, shards(): pl.pallas_call(result_kernel, out_shape=[jax.ShapeDtypeStruct((256, 1024)...  1.4 us

profile of v4, /device:TPU:1, one launch (start us, length us, event | category | flops | bytes accessed | tf_op | source)
XLA Modules:
  0.0 58.7 jit_solution(14978713745282066677)
XLA Ops:
  0.6 56.7 %shard_map.146 = (bf16[256,1024]{1,0:T(8,128)(2,1)S(1)}, bf16[256,3072]{1,0:T(8,128)(2,1)S(1)}, f32[8,16,128]{2,1,0:T(8,128)S(1)}, f32[64,512]{1,0:T(8,128)S(1)}) custom-call(bf16[256,3072]{1,0:T(8,128)(2,1)} %proj_h.1, bf16[256,1024]{1,0:T(8,128)(2,1)} %cot_h.1, f32[64,4096]{1,0:T(8,128)} %bitcast.4, f32[3,3072]{1,0:T(4,128)} %short_h.1, ...), custom_call_target="tpu_custom_call" | custom-call | tf_op jit(solution)/shard_map/pallas_call | solution.py:582
  57.3 1.4 %shard_map.147 = (bf16[256,1024]{1,0:T(8,128)(2,1)}, bf16[256,3072]{1,0:T(8,128)(2,1)}, f32[3,3072]{1,0:T(4,128)}, f32[1,1024]{1,0:T(1,128)}, f32[64,512]{1,0:T(8,128)}) custom-call(bf16[256,1024]{1,0:T(8,128)(2,1)S(1)} %get-tuple-element.14.out_v, bf16[256,3072]{1,0:T(8,128)(2,1)S(1)} %get-tuple-element.15.pg_v, ...), custom_call_target="tpu_custom_call" | custom-call | tf_op jit(solution)/shard_map/pallas_call | solution.py:642

commit v5 on v4

--- a/solution.py
+++ b/solution.py
@@ -225,7 +225,7 @@
 
         return carry
 
-    lax.fori_loop(0, 4, gate_tile, 0)
+    lax.fori_loop(0, 4, gate_tile, 0, unroll=2)
     half_wait(side)
     lax.fori_loop(4, 8, gate_tile, 0)
     for load in loads[2:]:
@@ -463,17 +463,12 @@
         return carry
 
     rsend_v[...] = jnp.zeros_like(rsend_v)
-    lax.fori_loop(0, 8, grad_tile, 0)
+    lax.fori_loop(0, 8, grad_tile, 0, unroll=2)
     rims = pltpu.make_async_remote_copy(
         src_ref=rsend_v, dst_ref=rrecv_v, send_sem=r_ss.at[0], recv_sem=r_rs.at[0],
         device_id={"ctx": prv}, device_id_type=MESH,
     )
-    rims.start()
     arecv_v[seat] = asend_v[seat]
-    whole_filter.wait_recv()
-    lax.fori_loop(0, 8, filter_half, 0)
-    half_filter.start()
-
     whole_sums = pltpu.make_async_remote_copy(
         src_ref=asend_v.at[pl.ds(0, 7)], dst_ref=arecv_v.at[pl.ds(0, 7)],
         send_sem=s_ss.at[0], recv_sem=s_rs.at[0], device_id={"ctx": nxt}, device_id_type=MESH,
@@ -500,8 +495,12 @@
     for step in range(1, 16):
         part_copy(lax.rem(line + step, 16), line).start()
 
+    rims.start()
+    whole_filter.wait_recv()
+    lax.fori_loop(0, 8, filter_half, 0)
+    half_filter.start()
+
     keep_back = jnp.where(me == 15, 0.0, 1.0).astype(F32)
-    rims.wait_recv()
 
     def last_tile(tile, carry):
         for part in range(3):
@@ -516,7 +515,6 @@
                 pg_v[pl.ds(top, CHUNK), cut] = value.astype(BF16)
         return carry
 
-    lax.fori_loop(0, 4, last_tile, 0)
 
     whole_parts = pltpu.make_async_remote_copy(
         src_ref=dsend_v.at[pl.ds(0, 15)], dst_ref=drecv_v.at[pl.ds(0, 15)],
@@ -532,7 +530,8 @@
     for step in range(1, 8):
         all_copy(lax.rem(seat + step, 8), seat).start()
 
-    lax.fori_loop(4, 8, last_tile, 0)
+    rims.wait_recv()
+    lax.fori_loop(0, 8, last_tile, 0)
     half_filter.wait_recv()
     for pair in range(8):
         value = filter_sum(pair, 32 * low_x) + hrecv_v[pair].astype(F32)

time: 58.9 us -> 58.4 us (level)
  no operation moved by 1% of the time
where the time goes in v5:
time: 58.4 us; the launch traced here: 58.3 us
  Pallas kernels  57.6 us (99%)
  between operations  0.64 us (1%)
    pallas_call x1, Pallas kernels, shards(): pl.pallas_call(functools.partial(kernel, scale), out_shape=[pltpu.VMEM((2...  56.2 us
    pallas_call x1, Pallas kernels, shards(): pl.pallas_call(result_kernel, out_shape=[jax.ShapeDtypeStruct((256, 1024)...  1.4 us

profile of v5, /device:TPU:1, one launch (start us, length us, event | category | flops | bytes accessed | tf_op | source)
XLA Modules:
  0.0 58.3 jit_solution(203034274494880680)
XLA Ops:
  0.6 56.2 %shard_map.146 = (bf16[256,1024]{1,0:T(8,128)(2,1)S(1)}, bf16[256,3072]{1,0:T(8,128)(2,1)S(1)}, f32[8,16,128]{2,1,0:T(8,128)S(1)}, f32[64,512]{1,0:T(8,128)S(1)}) custom-call(bf16[256,3072]{1,0:T(8,128)(2,1)} %proj_h.1, bf16[256,1024]{1,0:T(8,128)(2,1)} %cot_h.1, f32[64,4096]{1,0:T(8,128)} %bitcast.4, f32[3,3072]{1,0:T(4,128)} %short_h.1, ...), custom_call_target="tpu_custom_call" | custom-call | tf_op jit(solution)/shard_map/pallas_call | solution.py:581
  56.9 1.4 %shard_map.147 = (bf16[256,1024]{1,0:T(8,128)(2,1)}, bf16[256,3072]{1,0:T(8,128)(2,1)}, f32[3,3072]{1,0:T(4,128)}, f32[1,1024]{1,0:T(1,128)}, f32[64,512]{1,0:T(8,128)}) custom-call(bf16[256,1024]{1,0:T(8,128)(2,1)S(1)} %get-tuple-element.14.out_v, bf16[256,3072]{1,0:T(8,128)(2,1)S(1)} %get-tuple-element.15.pg_v, ...), custom_call_target="tpu_custom_call" | custom-call | tf_op jit(solution)/shard_map/pallas_call | solution.py:641
